TPU v7x, 32 devices: a whole 2x2x4 slice. The times are simulated.
32 devices in a mesh: tile: 16 (over z, y, core), scan: 2 (over x).
Axes of the slice: x: 2, y: 2, z: 4, core: 2. Of those that a mesh axis runs over, the one named last changes fastest.
Arguments:
- object_slab: float32 [2, 2, 1024, 512], P(None, None, 'tile', 'scan'), may hold values from -6 to 6
- probe_wave: bfloat16 [2, 512, 512], P(None, None, 'scan'), may hold values from -6 to 6
- amplitudes: float32 [32, 512, 512], P('tile', 'scan'), may hold values from 0.2 to 2
- row_offsets: int32 [32], P('tile'), may hold values from 0 to 63
- position_counts: int32 [16], P('tile'), may hold values from 0 to 2, as said below
Outputs:
- object_grad: float32 [2, 2, 1024, 512], P(None, None, 'tile', 'scan')
Inputs may be any that keep to these rules, and one draw needn't show every extreme that they name: position_counts is 1 to 2 on the first 8 tiles, equal to 2 on at least one of them, and 0 on the last 8 tiles.
All inputs are finite; a program needn't handle non-finite values.
Results may differ from a plain program's by a relative error of at most 0.0065.
Values may be sent and summed in bfloat16 or wider, within the bound.
No kernel may reach another device: no remote copies, remote signals or barrier semaphores. Data moves between devices by JAX's collectives and lax.ppermute only.
A program may use at most 64 MiB of HBM per device.

v0:
```python
import functools
import math

import jax
import jax.numpy as jnp
import ml_dtypes
import numpy as np
from jax import lax
from jax.experimental import pallas as pl
from jax.experimental.pallas import tpu as pltpu
from jax.sharding import PartitionSpec as P

fresnel = 0.5
smooth = 1.0
bf16 = jnp.bfloat16
f32 = jnp.float32


def tables(size):
    index = np.arange(size)
    angles = 2.0 * np.pi / size * (index[:, None] * index[None, :] % size)
    base = np.exp(1j * angles)
    far = np.conj(base) / math.sqrt(size)
    centred = np.where(index < size // 2, index, index - size).astype(np.float64)
    kernel = np.exp(-1j * np.pi * fresnel / size * centred * centred)
    near = (base * kernel[None, :]) @ np.conj(base).T / size

    def parts(table):
        stacked = np.stack([table.real, table.imag, -table.imag])
        return jnp.asarray(stacked.astype(ml_dtypes.bfloat16))

    order = np.concatenate([index[0::2], index[1::2]])
    return parts(far[order]), parts(far[:, order]), parts(near)


def left(table, conjugate, wave):
    real, plus, minus = table if not conjugate else (table[0], table[2], table[1])
    top = jnp.concatenate([real, minus], axis=1)
    bottom = jnp.concatenate([plus, real], axis=1)
    return (
        jnp.dot(top, wave, preferred_element_type=f32),
        jnp.dot(bottom, wave, preferred_element_type=f32),
    )


def right(table, conjugate, wave):
    real, plus, minus = table if not conjugate else (table[0], table[2], table[1])
    real_side = jnp.concatenate([real, minus], axis=0)
    imag_side = jnp.concatenate([plus, real], axis=0)
    return (
        jnp.dot(wave, real_side, preferred_element_type=f32),
        jnp.dot(wave, imag_side, preferred_element_type=f32),
    )


def one_hot(size, hit):
    row = lax.broadcasted_iota(jnp.int32, (size, size), 0)
    col = lax.broadcasted_iota(jnp.int32, (size, size), 1)
    return jnp.where(hit(row, col), 1.0, 0.0).astype(bf16)


def order_kernel(size, slot, measured, ordered, amps):
    half = size // 2
    if len(measured.shape) == 2:
        amps[...] = measured[...]
    else:
        for number in range(2):
            at = pl.multiple_of(jnp.where(slot[0] == number, 0, half), half)
            for side in range(2):
                cols = pl.ds(side * half, half)
                amps[pl.ds(at, half), cols] = measured[number, side]

    def frequency(place, natural):
        return natural == jnp.where(place < half, 2 * place, 2 * (place - half) + 1)

    rows_first = jnp.dot(one_hot(size, frequency), amps[...], preferred_element_type=f32)
    ordered[...] = jnp.dot(
        rows_first.astype(bf16),
        one_hot(size, lambda row, col: frequency(col, row)),
        preferred_element_type=f32,
    ).astype(bf16)


def in_order(measured, slot, size):
    whole = pl.BlockSpec(memory_space=pltpu.VMEM)
    return pl.pallas_call(
        functools.partial(order_kernel, size),
        out_shape=jax.ShapeDtypeStruct((size, size), bf16),
        in_specs=[pl.BlockSpec(memory_space=pltpu.SMEM), whole],
        out_specs=whole,
        scratch_shapes=[pltpu.VMEM((size, size), bf16)],
        compiler_params=pltpu.CompilerParams(vmem_limit_bytes=16 * 1024 * 1024),
        cost_estimate=pl.CostEstimate(
            flops=4 * size**3, bytes_accessed=4 * size * size, transcendentals=0
        ),
        name="in_order",
    )(slot, measured)


def roll_kernel(size, meta, far_rows, far_cols, *refs):
    pieces, (probe_out, near_side, far_side) = refs[:-3], refs[-3:]
    offset, slot = meta[0], meta[2]
    half = size // 2

    def moved(to, source):
        gap = to - source - offset
        return (gap == 0) | (gap == -size)

    down = one_hot(size, moved)
    across = one_hot(size, lambda row, col: moved(col, row))
    for c in range(3):
        near_side[c] = jnp.dot(
            far_rows[c], across[:, :half], preferred_element_type=f32
        ).astype(bf16)
        far_side[c] = jnp.dot(down[:half], far_cols[c], preferred_element_type=f32).astype(bf16)
    for c in range(2):
        done = 0
        for piece in pieces:
            turned = jnp.dot(down, piece[c, 0:size, :], preferred_element_type=f32).astype(bf16)
            width = turned.shape[1]
            if len(pieces) == 2:
                at = pl.multiple_of(jnp.where(slot == done, 0, width), width)
                probe_out[c, :, pl.ds(at, width)] = turned
                done += 1
            else:
                probe_out[c, :, done : done + width] = turned
                done += width


def rolled(pieces, far_rows, far_cols, meta, size):
    whole = pl.BlockSpec(memory_space=pltpu.VMEM)
    return pl.pallas_call(
        functools.partial(roll_kernel, size),
        out_shape=[
            jax.ShapeDtypeStruct((2, size, size), bf16),
            jax.ShapeDtypeStruct((3, size, size // 2), bf16),
            jax.ShapeDtypeStruct((3, size // 2, size), bf16),
        ],
        in_specs=[pl.BlockSpec(memory_space=pltpu.SMEM)] + [whole] * (2 + len(pieces)),
        out_specs=[whole] * 3,
        compiler_params=pltpu.CompilerParams(vmem_limit_bytes=24 * 1024 * 1024),
        cost_estimate=pl.CostEstimate(
            flops=64 * size**3, bytes_accessed=24 * size * size, transcendentals=0
        ),
        name="rolled",
    )(meta, far_rows, far_cols, *pieces)


def tile_access(size, span, tile_rows, meta, mine, theirs):
    offset, core = meta[0], meta[3]
    parts, _, width = mine.shape[1:]
    early = lax.broadcasted_iota(jnp.int32, (tile_rows, width), 0) < offset

    def place(k):
        return k // 2 if k % 2 == 0 else k // 2 + core

    def piece(k, h, s, c):
        source = mine if k % 2 == 0 else theirs
        at = (2 * s + c) * tile_rows
        return source[place(k), h, at : at + tile_rows, :].astype(f32)

    def patch(s, c):
        rows = []
        for k in range(span):
            blocks = [piece(k, h, s, c) for h in range(parts)]
            if k == 0:
                blocks = [jnp.where(early, piece(span, h, s, c), blocks[h]) for h in range(parts)]
            rows.append(jnp.concatenate(blocks, axis=1))
        return jnp.concatenate(rows, axis=0)

    return early, place, patch


def put_rows(rows_buf, pair):
    size = rows_buf.shape[1]
    for c in range(2):
        rows_buf[c * size : (c + 1) * size, :] = pair[c].astype(bf16)


def put_cols(cols_buf, pair):
    size = cols_buf.shape[0]
    for c in range(2):
        cols_buf[:, c * size : (c + 1) * size] = pair[c].astype(bf16)


def put_row_halves(rows_buf, first, second):
    half = rows_buf.shape[1] // 2
    for number, wave in enumerate((*first, *second)):
        rows_buf[number * half : (number + 1) * half, :] = wave.astype(bf16)


def put_col_halves(cols_buf, first, second):
    half = cols_buf.shape[0] // 2
    for number, wave in enumerate((*first, *second)):
        cols_buf[:, number * half : (number + 1) * half] = wave.astype(bf16)


def pair_of(ref):
    return ref[0].astype(f32), ref[1].astype(f32)


def parts_of(ref, rows, cols):
    return ref[0, rows, cols], ref[1, rows, cols], ref[2, rows, cols]


def both(first, second, axis):
    return [jnp.concatenate([a, b], axis=axis) for a, b in zip(first, second)]


def plus(first, second):
    return [a + b for a, b in zip(first, second)]


def less(first, second):
    return [a - b for a, b in zip(first, second)]


def forth_kernel(
    size, span, tile_rows, meta, mine, theirs, far_cols, near, probe, far_near,
    psi2, field, rows_buf, cols_buf,
):
    half = size // 2
    low, high, everything = slice(0, half), slice(half, size), slice(None)

    @pl.when(meta[1] == 1)
    def _():
        _, _, patch = tile_access(size, span, tile_rows, meta, mine, theirs)
        near_parts = parts_of(near, everything, everything)
        pr, pi = pair_of(probe)
        ar, ai = patch(0, 0), patch(0, 1)
        put_rows(rows_buf, (pr * ar - pi * ai, pr * ai + pi * ar))
        put_cols(cols_buf, left(near_parts, False, rows_buf[...]))
        two = right(near_parts, False, cols_buf[...])
        psi2[0] = two[0].astype(bf16)
        psi2[1] = two[1].astype(bf16)
        wr, wi = pair_of(psi2)
        br, bi = patch(1, 0), patch(1, 1)
        wave_exit = (wr * br - wi * bi, wr * bi + wi * br)
        top, bottom = [x[low] for x in wave_exit], [x[high] for x in wave_exit]
        put_row_halves(rows_buf, plus(top, bottom), less(top, bottom))
        half2 = both(
            left(parts_of(far_near, low, everything), False, rows_buf[0:size, :]),
            left(parts_of(far_near, high, everything), False, rows_buf[size : 2 * size, :]),
            0,
        )
        top, bottom = [x[:, low] for x in half2], [x[:, high] for x in half2]
        put_col_halves(cols_buf, plus(top, bottom), less(top, bottom))
        for cols, source in ((low, cols_buf[:, 0:size]), (high, cols_buf[:, size : 2 * size])):
            fr, fi = right(parts_of(far_cols, low, cols), False, source)
            field[0, :, cols] = fr
            field[1, :, cols] = fi


def back_kernel(
    size, span, tile_rows, meta, mine, theirs, far_rows, near, probe, far_far, amps, psi2, field,
    keep, send, rows_buf, cols_buf,
):
    core = meta[3]
    parts, _, _, _, width = keep.shape[1:]
    half = size // 2
    low, high, everything = slice(0, half), slice(half, size), slice(None)

    @pl.when(meta[1] == 1)
    def _():
        early, place, patch = tile_access(size, span, tile_rows, meta, mine, theirs)

        def put_term(s, c, term):
            for k in range(span):
                for h in range(parts):
                    block = term[
                        k * tile_rows : (k + 1) * tile_rows, h * width : (h + 1) * width
                    ]
                    if k == 0:
                        keep[place(span), h, s, c] = jnp.where(early, block, 0.0).astype(bf16)
                        block = jnp.where(early, 0.0, block)
                    target = keep if k % 2 == 0 else send
                    target[place(k), h, s, c] = block.astype(bf16)

        chis = []
        for cols in (low, high):
            fr, fi = field[0, :, cols], field[1, :, cols]
            keeping = 1.0 - amps[:, cols].astype(f32) * lax.rsqrt(fr * fr + fi * fi + smooth)
            chis.append((fr * keeping, fi * keeping))
        put_col_halves(cols_buf, *chis)
        even = right(parts_of(far_rows, low, low), True, cols_buf[:, 0:size])
        odd = right(parts_of(far_rows, high, low), True, cols_buf[:, size : 2 * size])
        back1 = both(plus(even, odd), less(even, odd), 1)
        put_row_halves(rows_buf, [x[low] for x in back1], [x[high] for x in back1])
        even = left(parts_of(far_far, everything, low), True, rows_buf[0:size, :])
        odd = left(parts_of(far_far, everything, high), True, rows_buf[size : 2 * size, :])
        er, ei = both(plus(even, odd), less(even, odd), 0)
        br, bi = patch(1, 0), patch(1, 1)
        put_cols(cols_buf, (br * er + bi * ei, br * ei - bi * er))
        wr, wi = pair_of(psi2)
        put_term(1, 0, wr * er + wi * ei)
        put_term(1, 1, wr * ei - wi * er)
        near_parts = parts_of(near, everything, everything)
        put_rows(rows_buf, right(near_parts, True, cols_buf[...]))
        gr, gi = left(near_parts, True, rows_buf[...])
        pr, pi = pair_of(probe)
        put_term(0, 0, pr * gr + pi * gi)
        put_term(0, 1, pr * gi - pi * gr)
        send[(1 - core) * (span // 2)] = jnp.zeros(send.shape[1:], bf16)

    @pl.when(meta[1] == 0)
    def _():
        keep[...] = jnp.zeros(keep.shape, bf16)
        send[...] = jnp.zeros(send.shape, bf16)


def kernel_call(kernel, size, tile_rows, name, flops, out_shape, meta, *inputs):
    inside = pl.BlockSpec(memory_space=pltpu.VMEM)
    return pl.pallas_call(
        functools.partial(kernel, size, size // tile_rows, tile_rows),
        out_shape=out_shape,
        in_specs=[pl.BlockSpec(memory_space=pltpu.SMEM)] + [inside] * len(inputs),
        out_specs=[inside] * len(out_shape),
        scratch_shapes=[
            pltpu.VMEM((2 * size, size), bf16),
            pltpu.VMEM((size, 2 * size), bf16),
        ],
        compiler_params=pltpu.CompilerParams(vmem_limit_bytes=36 * 1024 * 1024),
        cost_estimate=pl.CostEstimate(
            flops=flops, bytes_accessed=size * size, transcendentals=0
        ),
        name=name,
    )(meta, *inputs)


def shards(size, object_slab, probe_wave, amplitudes, row_offsets, position_counts):
    tile_rows = object_slab.shape[2]
    span = size // tile_rows
    count = lax.axis_size("tile")
    parts = lax.axis_size("scan")
    slots = amplitudes.shape[0]
    paired = parts == slots == 2
    slot = lax.axis_index("scan")
    ahead = span // 2
    homes = range(ahead, count - ahead)
    swap = [(0, 1), (1, 0)]

    def brought(value, steps):
        return lax.ppermute(value, "tile", [(home + steps, home) for home in homes])

    def returned(value, steps):
        return lax.ppermute(value, "tile", [(home, home + steps) for home in homes])

    def to_partner(value):
        return lax.ppermute(value, "tile", [(one, one ^ 1) for one in range(count)])

    def by_slot(first, second):
        return jnp.where(slot == 0, first, second)

    own = object_slab.astype(bf16)
    width = own.shape[-1]
    notes = jnp.concatenate([row_offsets, position_counts]).astype(bf16)
    notes = jnp.pad(notes[None], ((0, 15), (0, width - slots - 1)))

    def below(tile):
        return jnp.concatenate([tile.reshape((-1, width)), notes])

    if paired:
        beside = lax.ppermute(own, "scan", swap)
        whole = jnp.stack([below(by_slot(own, beside)), below(by_slot(beside, own))])

        def in_halves(value):
            return jnp.stack(jnp.split(value.astype(bf16), 2, axis=1))

        other = in_halves(by_slot(amplitudes[1], amplitudes[0]))
        got = lax.ppermute(jnp.concatenate([probe_wave, other], axis=1), "scan", swap)
        probe_pieces = [probe_wave, got]
        mine_amps = in_halves(by_slot(amplitudes[0], amplitudes[1]))
        measured = brought(jnp.stack([mine_amps, got[:, size:]]), -ahead)
    else:
        gathered = lax.all_gather(own, "scan")
        whole = jnp.stack([below(gathered[number]) for number in range(parts)])
        every = lax.all_gather(probe_wave, "scan")
        probe_pieces = [every[number] for number in range(parts)]
        every = lax.all_gather(brought(amplitudes.astype(bf16), -ahead), "scan")
        measured = every[:, jnp.minimum(slot, slots - 1)].reshape((size, size))
    far_rows, far_cols, near = tables(size)
    steps = range(-ahead, ahead + 1, 2)
    arrived = {0: whole}
    for step in sorted(steps, key=abs)[1:]:
        arrived[step] = brought(whole, step)
    notes = arrived[-ahead][0, -16, : slots + 1].astype(jnp.int32)
    live = (slot < notes[slots]).astype(jnp.int32)
    core = lax.rem(lax.axis_index("tile"), 2)
    meta = jnp.stack(
        [notes[jnp.minimum(slot, slots - 1)], live, slot.astype(jnp.int32), core.astype(jnp.int32)]
    )
    turned, far_near, far_far = rolled(probe_pieces, far_rows, far_cols, meta, size)
    mine = jnp.stack([arrived[step] for step in steps])
    theirs = to_partner(mine)
    shape = jax.ShapeDtypeStruct
    psi2, field = kernel_call(
        forth_kernel, size, tile_rows, "forth", 24 * size**3,
        [shape((2, size, size), bf16), shape((2, size, size), f32)],
        meta, mine, theirs, far_cols, near, turned, far_near,
    )
    measured, field = lax.optimization_barrier((measured, field))
    amps = in_order(measured, slot.astype(jnp.int32)[None], size)
    keep, send = kernel_call(
        back_kernel, size, tile_rows, "back", 24 * size**3,
        [shape((len(steps), parts, 2, 2, tile_rows, width), bf16)] * 2,
        meta, mine, theirs, far_rows, near, turned, far_far, amps, psi2, field,
    )
    merged = (keep.astype(f32) + to_partner(send).astype(f32)).astype(bf16)
    total = sum(
        (returned(merged[steps.index(step)], step) if step else merged[ahead // 2]).astype(f32)
        for step in (2, -ahead, ahead, -2, 0)
    )
    if paired:
        away = lax.ppermute(by_slot(total[1], total[0]).astype(bf16), "scan", swap)
        return by_slot(total[0], total[1]) + away.astype(f32)
    return lax.psum_scatter(total, "scan", scatter_dimension=0, tiled=False)


def solution(mesh):
    in_specs = (
        P(None, None, "tile", "scan"),
        P(None, None, "scan"),
        P("tile", "scan", None),
        P("tile"),
        P("tile"),
    )
    out_specs = P(None, None, "tile", "scan")

    def run(object_slab, *rest):
        return jax.shard_map(
            functools.partial(shards, object_slab.shape[3]),
            mesh=mesh, in_specs=in_specs, out_specs=out_specs, check_vma=False,
        )(object_slab, *rest)

    return run
```

profile of v0, /device:TPU:0, one launch (start us, length us, event | category | flops | bytes accessed | tf_op | source)
XLA Modules:
  0.0 86.0 jit_solution(5264800250449600481)
XLA Ops:
  0.0 1.0 %convert_element_type.66 = bf16[2,2,64,256]{3,2,1,0:T(8,128)(2,1)S(1)} convert(f32[2,2,64,256]{3,2,1,0:T(8,128)} %param.8) | non-fusion elementwise | flops 65536 | bytes 393216 | tf_op jit(solution)/shard_map/convert_element_type | solution.py:354
  1.0 3.0 %collective-permute-start = (bf16[2,2,64,256]{3,2,1,0:T(8,128)(2,1)S(1)}, bf16[2,2,64,256]{3,2,1,0:T(8,128)(2,1)S(1)}, u32[]{:S(2)}, u32[]{:S(2)}) collective-permute-start(bf16[2,2,64,256]{3,2,1,0:T(8,128)(2,1)S(1)} %convert_element_type.66), channel_id=1, source_target_pairs={{0,1},{1,0},{2,3},{3,2},{4,5},{5,4},{6,7},{7,6},{8,9},{9,8},{10,11... | collective-permute-start | bytes 393224 | tf_op jit(solution)/shard_map/ppermute | solution.py:363
  4.0 1.3 %fusion.1 = (bf16[256,512]{1,0:T(8,128)(2,1)S(1)}, bf16[256,512]{1,0:T(8,128)(2,1)S(1)}) fusion(f32[2,256,512]{2,1,0:T(8,128)} %param.10, pred[]{:T(512)S(6)} %eq.2), kind=kLoop, calls=%fused_computation.13 | loop fusion | flops 262144 | bytes 1048577 | tf_op jit(solution)/shard_map/convert_element_type | solution.py:367
  6.1 1.5 %collective-permute-done = bf16[2,2,64,256]{3,2,1,0:T(8,128)(2,1)S(1)} collective-permute-done((bf16[2,2,64,256]{3,2,1,0:T(8,128)(2,1)S(1)}, bf16[2,2,64,256]{3,2,1,0:T(8,128)(2,1)S(1)}, u32[]{:S(2)}, u32[]{:S(2)}) %collective-permute-start) | collective-permute-done | bytes 131104 | tf_op jit(solution)/shard_map/ppermute | solution.py:363
  7.6 0.7 pad_maximum_fusion.1
  8.3 3.7 %collective-permute-start.1 = (bf16[2,272,256]{2,1,0:T(8,128)(2,1)}, bf16[2,272,256]{2,1,0:T(8,128)(2,1)S(1)}, u32[]{:S(2)}, u32[]{:S(2)}) collective-permute-start(bf16[2,272,256]{2,1,0:T(8,128)(2,1)} %pad_maximum_fusion.1), channel_id=1, source_target_pairs={{0,8},{2,10},{4,12},{6,14},{8,16},{10,18},{12,20},{14,22},{1,9},{3... | collective-permute-start | bytes 835592 | tf_op jit(solution)/shard_map/ppermute | solution.py:343
  12.1 0.9 %maximum_maximum_fusion = bf16[2,768,256]{2,1,0:T(8,128)(2,1)} fusion(bf16[1,256,256]{2,1,0:T(8,128)(2,1)S(1)} %get-tuple-element.39, bf16[1,256,256]{2,1,0:T(8,128)(2,1)S(1)} %get-tuple-element.40, bf16[2,512,256]{2,1,0:T(8,128)(2,1)S(1)} %copy-done), kind=kLoop, calls=%fused_computation.1 | loop fusion | flops 2359296 | bytes 1572864 | tf_op jit(solution)/shard_map/concatenate | solution.py:370
  13.1 1.5 %collective-permute-start.6 = (bf16[2,768,256]{2,1,0:T(8,128)(2,1)}, bf16[2,768,256]{2,1,0:T(8,128)(2,1)S(1)}, u32[]{:S(2)}, u32[]{:S(2)}) collective-permute-start(bf16[2,768,256]{2,1,0:T(8,128)(2,1)} %maximum_maximum_fusion), channel_id=1, source_target_pairs={{0,1},{1,0},{2,3},{3,2},{4,5},{5,4},{6,7},{7,6},{8,9},{9,8},{10,11... | collective-permute-start | bytes 2359304 | tf_op jit(solution)/shard_map/ppermute | solution.py:370
  14.6 1.4 %collective-permute-start.2 = (bf16[2,272,256]{2,1,0:T(8,128)(2,1)}, bf16[2,272,256]{2,1,0:T(8,128)(2,1)}, u32[]{:S(2)}, u32[]{:S(2)}) collective-permute-start(bf16[2,272,256]{2,1,0:T(8,128)(2,1)} %pad_maximum_fusion.1), channel_id=1, source_target_pairs={{4,8},{6,10},{8,12},{10,14},{12,16},{14,18},{16,20},{18,22},{5,9},... | collective-permute-start | bytes 835592 | tf_op jit(solution)/shard_map/ppermute | solution.py:343
  16.0 0.7 collective-permute-start.3
  16.7 0.7 collective-permute-start.4
  17.4 1.0 %bitcast_dynamic-update-slice_fusion.3 = bf16[5,2,272,256]{3,2,1,0:T(8,128)(2,1)S(1)} fusion(bf16[5,2,272,256]{3,2,1,0:T(8,128)(2,1)S(1)} %bitcast_dynamic-update-slice_fusion.4, bf16[2,272,256]{2,1,0:T(8,128)(2,1)} %collective-permute-done.2), kind=kLoop, calls=%fused_computation.10 | loop fusion | bytes 557056
  18.6 0.7 constant_dynamic-slice_fusion
  20.0 0.9 %pad_add_fusion.meta = s32[4]{0:T(128)S(1)} fusion(s32[1]{0:T(128)} %bitcast.10, s32[1]{0:T(128)} %bitcast.9.slot, s32[1]{0:T(128)} %bitcast.8, s32[1]{0:T(128)} %bitcast.6), kind=kLoop, calls=%fused_computation.43 | loop fusion | flops 12 | bytes 32 | tf_op jit(solution)/shard_map/stack | solution.py:389
  20.9 10.5 %collective-permute-done.6.refs_1_ = bf16[2,768,256]{2,1,0:T(8,128)(2,1)S(1)} collective-permute-done((bf16[2,768,256]{2,1,0:T(8,128)(2,1)}, bf16[2,768,256]{2,1,0:T(8,128)(2,1)S(1)}, u32[]{:S(2)}, u32[]{:S(2)}) %collective-permute-start.6) | collective-permute-done | bytes 786464 | tf_op jit(solution)/shard_map/ppermute | solution.py:370
  31.5 7.2 %collective-permute-start.7 = (bf16[2,2,256,256]{3,2,1,0:T(8,128)(2,1)S(1)}, bf16[2,2,256,256]{3,2,1,0:T(8,128)(2,1)S(1)}, u32[]{:S(2)}, u32[]{:S(2)}) collective-permute-start(bf16[2,2,256,256]{3,2,1,0:T(8,128)(2,1)S(1)} %pad_maximum_fusion), channel_id=1, source_target_pairs={{0,8},{2,10},{4,12},{6,14},{8,16},{10,18},{12,20},{14,22},{1,9},{3... | collective-permute-start | bytes 1572872 | tf_op jit(solution)/shard_map/ppermute | solution.py:343
  38.7 1.4 %copy-done.3 = bf16[3,512,512]{2,1,0:T(8,128)(2,1)S(1)} copy-done((bf16[3,512,512]{2,1,0:T(8,128)(2,1)S(1)}, bf16[3,512,512]{2,1,0:T(8,128)(2,1)}, u32[]{:S(2)}) %copy-start.3) | copy-done | bytes 1572888
  40.1 2.1 %rolled.1 = (bf16[2,512,512]{2,1,0:T(8,128)(2,1)S(1)}, bf16[3,512,256]{2,1,0:T(8,128)(2,1)S(1)}, bf16[3,256,512]{2,1,0:T(8,128)(2,1)S(1)}) custom-call(s32[4]{0:T(128)S(1)} %pad_add_fusion.meta, bf16[3,512,512]{2,1,0:T(8,128)(2,1)S(1)} %copy-done.1, bf16[3,512,512]{2,1,0:T(8,128)(2,1)S(1)} %copy-done.3, bf16[2,512,256]{2,1,0:T(8,128)(2,1)S(1)} %copy-done, ...), custom_call_target="tpu_custom_call" | custom-call | flops 8589934592 | bytes 6291456 | tf_op jit(solution)/shard_map/rolled/pallas_call | solution.py:132
  42.3 1.4 %forth.1 = (bf16[2,512,512]{2,1,0:T(8,128)(2,1)S(1)}, f32[2,512,512]{2,1,0:T(8,128)S(1)}) custom-call(s32[4]{0:T(128)S(1)} %pad_add_fusion.meta, bf16[5,2,272,256]{3,2,1,0:T(8,128)(2,1)S(1)} %bitcast_dynamic-update-slice_fusion.mine, bf16[5,2,272,256]{3,2,1,0:T(8,128)(2,1)} %collective-permute-done.5.theirs, bf16[3,512,512]{2,1,0:T(8,128)(2,1)S(1)} %copy-done.4, ...), custom_call_target="tpu_custom_call" | custom-call | flops 3221225472 | bytes 262144 | tf_op jit(solution)/shard_map/forth/pallas_call | solution.py:313
  43.7 6.8 %collective-permute-done.7.measured = bf16[2,2,256,256]{3,2,1,0:T(8,128)(2,1)S(1)} collective-permute-done((bf16[2,2,256,256]{3,2,1,0:T(8,128)(2,1)S(1)}, bf16[2,2,256,256]{3,2,1,0:T(8,128)(2,1)S(1)}, u32[]{:S(2)}, u32[]{:S(2)}) %collective-permute-start.7) | collective-permute-done | bytes 524320 | tf_op jit(solution)/shard_map/ppermute | solution.py:343
  50.5 0.8 in_order.1.amps
  51.3 1.5 %back.1 = (bf16[5,2,2,2,64,256]{5,4,3,2,1,0:T(8,128)(2,1)S(1)}, bf16[5,2,2,2,64,256]{5,4,3,2,1,0:T(8,128)(2,1)S(1)}) custom-call(s32[4]{0:T(128)S(1)} %pad_add_fusion.meta, bf16[5,2,272,256]{3,2,1,0:T(8,128)(2,1)S(1)} %bitcast_dynamic-update-slice_fusion.mine, bf16[5,2,272,256]{3,2,1,0:T(8,128)(2,1)} %collective-permute-done.5.theirs, ...), custom_call_target="tpu_custom_call" | custom-call | flops 3221225472 | bytes 262144 | tf_op jit(solution)/shard_map/back/pallas_call | solution.py:313
  52.9 3.0 %collective-permute-done.8 = bf16[5,2,2,2,64,256]{5,4,3,2,1,0:T(8,128)(2,1)S(1)} collective-permute-done((bf16[5,2,2,2,64,256]{5,4,3,2,1,0:T(8,128)(2,1)S(1)}, bf16[5,2,2,2,64,256]{5,4,3,2,1,0:T(8,128)(2,1)S(1)}, u32[]{:S(2)}, u32[]{:S(2)}) %collective-permute-start.8) | collective-permute-done | bytes 1310752 | tf_op jit(solution)/shard_map/ppermute | solution.py:349
  55.9 0.5 add_convert_fusion
  56.5 0.7 collective-permute-start.9
  57.2 0.7 collective-permute-start.12
  57.9 0.7 collective-permute-start.11
  58.6 1.3 %collective-permute-start.10 = (bf16[2,2,2,64,256]{4,3,2,1,0:T(8,128)(2,1)S(1)}, bf16[2,2,2,64,256]{4,3,2,1,0:T(8,128)(2,1)S(1)}, u32[]{:S(2)}, u32[]{:S(2)}) collective-permute-start(bf16[2,2,2,64,256]{4,3,2,1,0:T(8,128)(2,1)S(1)} %get-tuple-element.26), channel_id=1, source_target_pairs={{8,0},{10,2},{12,4},{14,6},{16,8},{18,10},{20,12},{22,14},{9,1},{1... | collective-permute-start | bytes 786440 | tf_op jit(solution)/shard_map/ppermute | solution.py:346
  59.9 20.1 %collective-permute-done.10 = bf16[2,2,2,64,256]{4,3,2,1,0:T(8,128)(2,1)S(1)} collective-permute-done((bf16[2,2,2,64,256]{4,3,2,1,0:T(8,128)(2,1)S(1)}, bf16[2,2,2,64,256]{4,3,2,1,0:T(8,128)(2,1)S(1)}, u32[]{:S(2)}, u32[]{:S(2)}) %collective-permute-start.10) | collective-permute-done | bytes 262176 | tf_op jit(solution)/shard_map/ppermute | solution.py:346
  80.2 0.6 collective-permute-start.13
  80.8 4.4 %collective-permute-done.13 = bf16[2,2,64,256]{3,2,1,0:T(8,128)(2,1)S(1)} collective-permute-done((bf16[2,2,64,256]{3,2,1,0:T(8,128)(2,1)S(1)}, bf16[2,2,64,256]{3,2,1,0:T(8,128)(2,1)S(1)}, u32[]{:S(2)}, u32[]{:S(2)}) %collective-permute-start.13) | collective-permute-done | bytes 131104 | tf_op jit(solution)/shard_map/ppermute | solution.py:414
  85.2 0.8 bitcast_add_fusion
  (39 shorter events, 0.9 us)
Async XLA Ops:
  0.0 7.5 %copy-start.5 = (f32[2,2,64,256]{3,2,1,0:T(8,128)S(1)}, f32[2,2,64,256]{3,2,1,0:T(8,128)}, u32[]{:S(2)}) copy-start(f32[2,2,64,256]{3,2,1,0:T(8,128)} %param.8) | copy-start | bytes 786436
  0.0 5.3 %copy-start.6 = (s32[2]{0:T(128)S(1)}, s32[2]{0:T(128)}, u32[]{:S(2)}) copy-start(s32[2]{0:T(128)} %param.11) | copy-start | bytes 28
  1.0 6.5 %collective-permute-start = (bf16[2,2,64,256]{3,2,1,0:T(8,128)(2,1)S(1)}, bf16[2,2,64,256]{3,2,1,0:T(8,128)(2,1)S(1)}, u32[]{:S(2)}, u32[]{:S(2)}) collective-permute-start(bf16[2,2,64,256]{3,2,1,0:T(8,128)(2,1)S(1)} %convert_element_type.66), channel_id=1, source_target_pairs={{0,1},{1,0},{2,3},{3,2},{4,5},{5,4},{6,7},{7,6},{8,9},{9,8},{10,11... | collective-permute-start | bytes 393224 | tf_op jit(solution)/shard_map/ppermute | solution.py:363
  6.1 6.1 %copy-start = (bf16[2,512,256]{2,1,0:T(8,128)(2,1)S(1)}, bf16[2,512,256]{2,1,0:T(8,128)(2,1)}, u32[]{:S(2)}) copy-start(bf16[2,512,256]{2,1,0:T(8,128)(2,1)} %refs_0_.1) | copy-start | bytes 1572868
  8.3 9.1 %collective-permute-start.1 = (bf16[2,272,256]{2,1,0:T(8,128)(2,1)}, bf16[2,272,256]{2,1,0:T(8,128)(2,1)S(1)}, u32[]{:S(2)}, u32[]{:S(2)}) collective-permute-start(bf16[2,272,256]{2,1,0:T(8,128)(2,1)} %pad_maximum_fusion.1), channel_id=1, source_target_pairs={{0,8},{2,10},{4,12},{6,14},{8,16},{10,18},{12,20},{14,22},{1,9},{3... | collective-permute-start | bytes 835592 | tf_op jit(solution)/shard_map/ppermute | solution.py:343
  13.1 18.3 %collective-permute-start.6 = (bf16[2,768,256]{2,1,0:T(8,128)(2,1)}, bf16[2,768,256]{2,1,0:T(8,128)(2,1)S(1)}, u32[]{:S(2)}, u32[]{:S(2)}) collective-permute-start(bf16[2,768,256]{2,1,0:T(8,128)(2,1)} %maximum_maximum_fusion), channel_id=1, source_target_pairs={{0,1},{1,0},{2,3},{3,2},{4,5},{5,4},{6,7},{7,6},{8,9},{9,8},{10,11... | collective-permute-start | bytes 2359304 | tf_op jit(solution)/shard_map/ppermute | solution.py:370
  14.6 2.9 %collective-permute-start.2 = (bf16[2,272,256]{2,1,0:T(8,128)(2,1)}, bf16[2,272,256]{2,1,0:T(8,128)(2,1)}, u32[]{:S(2)}, u32[]{:S(2)}) collective-permute-start(bf16[2,272,256]{2,1,0:T(8,128)(2,1)} %pad_maximum_fusion.1), channel_id=1, source_target_pairs={{4,8},{6,10},{8,12},{10,14},{12,16},{14,18},{16,20},{18,22},{5,9},... | collective-permute-start | bytes 835592 | tf_op jit(solution)/shard_map/ppermute | solution.py:343
  16.0 2.5 %collective-permute-start.3 = (bf16[2,272,256]{2,1,0:T(8,128)(2,1)}, bf16[2,272,256]{2,1,0:T(8,128)(2,1)S(1)}, u32[]{:S(2)}, u32[]{:S(2)}) collective-permute-start(bf16[2,272,256]{2,1,0:T(8,128)(2,1)} %pad_maximum_fusion.1), channel_id=1, source_target_pairs={{12,8},{14,10},{16,12},{18,14},{20,16},{22,18},{24,20},{26,22},{13... | collective-permute-start | bytes 835592 | tf_op jit(solution)/shard_map/ppermute | solution.py:343
  16.7 1.8 %collective-permute-start.4 = (bf16[2,272,256]{2,1,0:T(8,128)(2,1)}, bf16[2,272,256]{2,1,0:T(8,128)(2,1)S(1)}, u32[]{:S(2)}, u32[]{:S(2)}) collective-permute-start(bf16[2,272,256]{2,1,0:T(8,128)(2,1)} %pad_maximum_fusion.1), channel_id=1, source_target_pairs={{16,8},{18,10},{20,12},{22,14},{24,16},{26,18},{28,20},{30,22},{17... | collective-permute-start | bytes 835592 | tf_op jit(solution)/shard_map/ppermute | solution.py:343
  18.5 23.7 %collective-permute-start.5 = (bf16[5,2,272,256]{3,2,1,0:T(8,128)(2,1)S(1)}, bf16[5,2,272,256]{3,2,1,0:T(8,128)(2,1)}, u32[]{:S(2)}, u32[]{:S(2)}) collective-permute-start(bf16[5,2,272,256]{3,2,1,0:T(8,128)(2,1)S(1)} %bitcast_dynamic-update-slice_fusion.mine), channel_id=1, source_target_pairs={{0,2},{2,0},{4,6},{6,4},{8,10},{10,8},{12,14},{14,12},{16,18},{18,... | collective-permute-start | bytes 4177928 | tf_op jit(solution)/shard_map/ppermute | solution.py:349
  20.0 18.7 %copy-start.1 = (bf16[3,512,512]{2,1,0:T(8,128)(2,1)S(1)}, bf16[3,512,512]{2,1,0:T(8,128)(2,1)}, u32[]{:S(2)}) copy-start(bf16[3,512,512]{2,1,0:T(8,128)(2,1)} %constant.26.clone.far_rows) | copy-start | bytes 4718596
  31.5 10.8 %copy-start.2 = (bf16[3,512,512]{2,1,0:T(8,128)(2,1)S(1)}, bf16[3,512,512]{2,1,0:T(8,128)(2,1)}, u32[]{:S(2)}) copy-start(bf16[3,512,512]{2,1,0:T(8,128)(2,1)} %constant.28.clone.near) | copy-start | bytes 4718596
  31.5 19.0 %collective-permute-start.7 = (bf16[2,2,256,256]{3,2,1,0:T(8,128)(2,1)S(1)}, bf16[2,2,256,256]{3,2,1,0:T(8,128)(2,1)S(1)}, u32[]{:S(2)}, u32[]{:S(2)}) collective-permute-start(bf16[2,2,256,256]{3,2,1,0:T(8,128)(2,1)S(1)} %pad_maximum_fusion), channel_id=1, source_target_pairs={{0,8},{2,10},{4,12},{6,14},{8,16},{10,18},{12,20},{14,22},{1,9},{3... | collective-permute-start | bytes 1572872 | tf_op jit(solution)/shard_map/ppermute | solution.py:343
  38.7 1.4 %copy-start.3 = (bf16[3,512,512]{2,1,0:T(8,128)(2,1)S(1)}, bf16[3,512,512]{2,1,0:T(8,128)(2,1)}, u32[]{:S(2)}) copy-start(bf16[3,512,512]{2,1,0:T(8,128)(2,1)} %constant.27.clone.far_cols) | copy-start | bytes 4718596
  40.1 2.2 %copy-start.4 = (bf16[3,512,512]{2,1,0:T(8,128)(2,1)S(1)}, bf16[3,512,512]{2,1,0:T(8,128)(2,1)}, u32[]{:S(2)}) copy-start(bf16[3,512,512]{2,1,0:T(8,128)(2,1)} %constant.27.clone.far_cols) | copy-start | bytes 4718596
  52.8 3.1 %collective-permute-start.8 = (bf16[5,2,2,2,64,256]{5,4,3,2,1,0:T(8,128)(2,1)S(1)}, bf16[5,2,2,2,64,256]{5,4,3,2,1,0:T(8,128)(2,1)S(1)}, u32[]{:S(2)}, u32[]{:S(2)}) collective-permute-start(bf16[5,2,2,2,64,256]{5,4,3,2,1,0:T(8,128)(2,1)S(1)} %get-tuple-element.22), channel_id=1, source_target_pairs={{0,2},{2,0},{4,6},{6,4},{8,10},{10,8},{12,14},{14,12},{16,18},{18,... | collective-permute-start | bytes 3932168 | tf_op jit(solution)/shard_map/ppermute | solution.py:349
  56.5 3.4 %collective-permute-start.9 = (bf16[2,2,2,64,256]{4,3,2,1,0:T(8,128)(2,1)S(1)}, bf16[2,2,2,64,256]{4,3,2,1,0:T(8,128)(2,1)S(1)}, u32[]{:S(2)}, u32[]{:S(2)}) collective-permute-start(bf16[2,2,2,64,256]{4,3,2,1,0:T(8,128)(2,1)S(1)} %get-tuple-element.23), channel_id=1, source_target_pairs={{8,12},{10,14},{12,16},{14,18},{16,20},{18,22},{20,24},{22,26},{9,... | collective-permute-start | bytes 786440 | tf_op jit(solution)/shard_map/ppermute | solution.py:346
  57.2 2.7 %collective-permute-start.12 = (bf16[2,2,2,64,256]{4,3,2,1,0:T(8,128)(2,1)S(1)}, bf16[2,2,2,64,256]{4,3,2,1,0:T(8,128)(2,1)S(1)}, u32[]{:S(2)}, u32[]{:S(2)}) collective-permute-start(bf16[2,2,2,64,256]{4,3,2,1,0:T(8,128)(2,1)S(1)} %get-tuple-element.24), channel_id=1, source_target_pairs={{8,4},{10,6},{12,8},{14,10},{16,12},{18,14},{20,16},{22,18},{9,5},... | collective-permute-start | bytes 786440 | tf_op jit(solution)/shard_map/ppermute | solution.py:346
  57.9 2.0 %collective-permute-start.11 = (bf16[2,2,2,64,256]{4,3,2,1,0:T(8,128)(2,1)S(1)}, bf16[2,2,2,64,256]{4,3,2,1,0:T(8,128)(2,1)S(1)}, u32[]{:S(2)}, u32[]{:S(2)}) collective-permute-start(bf16[2,2,2,64,256]{4,3,2,1,0:T(8,128)(2,1)S(1)} %get-tuple-element.25), channel_id=1, source_target_pairs={{8,16},{10,18},{12,20},{14,22},{16,24},{18,26},{20,28},{22,30},{9,... | collective-permute-start | bytes 786440 | tf_op jit(solution)/shard_map/ppermute | solution.py:346
  58.6 21.4 %collective-permute-start.10 = (bf16[2,2,2,64,256]{4,3,2,1,0:T(8,128)(2,1)S(1)}, bf16[2,2,2,64,256]{4,3,2,1,0:T(8,128)(2,1)S(1)}, u32[]{:S(2)}, u32[]{:S(2)}) collective-permute-start(bf16[2,2,2,64,256]{4,3,2,1,0:T(8,128)(2,1)S(1)} %get-tuple-element.26), channel_id=1, source_target_pairs={{8,0},{10,2},{12,4},{14,6},{16,8},{18,10},{20,12},{22,14},{9,1},{1... | collective-permute-start | bytes 786440 | tf_op jit(solution)/shard_map/ppermute | solution.py:346
  80.2 5.0 %collective-permute-start.13 = (bf16[2,2,64,256]{3,2,1,0:T(8,128)(2,1)S(1)}, bf16[2,2,64,256]{3,2,1,0:T(8,128)(2,1)S(1)}, u32[]{:S(2)}, u32[]{:S(2)}) collective-permute-start(bf16[2,2,64,256]{3,2,1,0:T(8,128)(2,1)S(1)} %fusion.4), channel_id=1, source_target_pairs={{0,1},{1,0},{2,3},{3,2},{4,5},{5,4},{6,7},{7,6},{8,9},{9,8},{10,11... | collective-permute-start | bytes 393224 | tf_op jit(solution)/shard_map/ppermute | solution.py:414
where the time goes:
time: 86.5 us; the launch traced here: 86 us
  waiting for transfers between devices  46.5 us (54%)
  starting transfers between devices  22.2 us (26%)
  other arithmetic  6.55 us (8%)
  Pallas kernels  5.81 us (7%)
  local copies, waits for them, and re-layouts  3.26 us (4%)
  between operations  1.71 us (2%)
    ppermute x4, waiting for transfers between devices, returned(): return lax.ppermute(value, 'tile', [(home, home + steps) for home in homes])  20.1 us
    ppermute x5, starting transfers between devices, brought(): return lax.ppermute(value, 'tile', [(home + steps, home) for home in homes])  13.6 us
    ppermute x1, waiting for transfers between devices, shards(): lax.ppermute(jnp.concatenate([probe_wave, other], axis=1), 'scan', swap)  10.5 us
    ppermute x5, waiting for transfers between devices, brought(): return lax.ppermute(value, 'tile', [(home + steps, home) for home in homes])  6.88 us
    ppermute x1, waiting for transfers between devices, shards(): away = lax.ppermute(by_slot(total[1], total[0]).astype(bf16), 'scan', swap)  4.45 us
    ppermute x4, starting transfers between devices, returned(): return lax.ppermute(value, 'tile', [(home, home + steps) for home in homes])  3.32 us
    ppermute x2, waiting for transfers between devices, to_partner(): return lax.ppermute(value, 'tile', [(one, one ^ 1) for one in range(count)])  3.02 us
    ppermute x1, starting transfers between devices, shards(): beside = lax.ppermute(own, 'scan', swap)  3 us
  transfers between devices with their start and end apart: 14, of which 7 were waited for; matrix products, arithmetic and copies ran while one was open for 6% of the time, Pallas kernels for 4%

commit v1 on v0

--- a/solution.py
+++ b/solution.py
@@ -59,16 +59,13 @@
     return jnp.where(hit(row, col), 1.0, 0.0).astype(bf16)
 
 
-def order_kernel(size, slot, measured, ordered, amps):
+def order_kernel(size, slot, *refs):
+    measured, (ordered, amps) = refs[:-2], refs[-2:]
     half = size // 2
-    if len(measured.shape) == 2:
-        amps[...] = measured[...]
-    else:
-        for number in range(2):
-            at = pl.multiple_of(jnp.where(slot[0] == number, 0, half), half)
-            for side in range(2):
-                cols = pl.ds(side * half, half)
-                amps[pl.ds(at, half), cols] = measured[number, side]
+    for number, piece in enumerate(measured):
+        rows = piece.shape[0]
+        at = pl.multiple_of(jnp.where(slot[0] == number, 0, size - rows), rows)
+        amps[pl.ds(at, rows), :] = piece[...]
 
     def frequency(place, natural):
         return natural == jnp.where(place < half, 2 * place, 2 * (place - half) + 1)
@@ -86,7 +83,7 @@
     return pl.pallas_call(
         functools.partial(order_kernel, size),
         out_shape=jax.ShapeDtypeStruct((size, size), bf16),
-        in_specs=[pl.BlockSpec(memory_space=pltpu.SMEM), whole],
+        in_specs=[pl.BlockSpec(memory_space=pltpu.SMEM)] + [whole] * len(measured),
         out_specs=whole,
         scratch_shapes=[pltpu.VMEM((size, size), bf16)],
         compiler_params=pltpu.CompilerParams(vmem_limit_bytes=16 * 1024 * 1024),
@@ -94,7 +91,7 @@
             flops=4 * size**3, bytes_accessed=4 * size * size, transcendentals=0
         ),
         name="in_order",
-    )(slot, measured)
+    )(slot, *measured)
 
 
 def roll_kernel(size, meta, far_rows, far_cols, *refs):
@@ -116,7 +113,7 @@
     for c in range(2):
         done = 0
         for piece in pieces:
-            turned = jnp.dot(down, piece[c, 0:size, :], preferred_element_type=f32).astype(bf16)
+            turned = jnp.dot(down, piece[c], preferred_element_type=f32).astype(bf16)
             width = turned.shape[1]
             if len(pieces) == 2:
                 at = pl.multiple_of(jnp.where(slot == done, 0, width), width)
@@ -342,14 +339,23 @@
     def brought(value, steps):
         return lax.ppermute(value, "tile", [(home + steps, home) for home in homes])
 
-    def returned(value, steps):
-        return lax.ppermute(value, "tile", [(home, home + steps) for home in homes])
-
-    def to_partner(value):
-        return lax.ppermute(value, "tile", [(one, one ^ 1) for one in range(count)])
+    def paired_with(value, unit):
+        return lax.ppermute(value, "tile", [(one, one ^ unit) for one in range(count)])
+
+    def paired_across(value, unit):
+        pairs = []
+        for one in range(unit, count - unit):
+            step = unit if (one // unit) % 2 else -unit
+            pairs.append((one, one + step))
+        return lax.ppermute(value, "tile", pairs)
 
     def by_slot(first, second):
         return jnp.where(slot == 0, first, second)
+
+    tile = lax.axis_index("tile")
+
+    def by_place(unit, if_odd, if_even):
+        return jnp.where((tile // unit) % 2 == 1, if_odd, if_even)
 
     own = object_slab.astype(bf16)
     width = own.shape[-1]
@@ -363,52 +369,68 @@
         beside = lax.ppermute(own, "scan", swap)
         whole = jnp.stack([below(by_slot(own, beside)), below(by_slot(beside, own))])
 
-        def in_halves(value):
-            return jnp.stack(jnp.split(value.astype(bf16), 2, axis=1))
-
-        other = in_halves(by_slot(amplitudes[1], amplitudes[0]))
-        got = lax.ppermute(jnp.concatenate([probe_wave, other], axis=1), "scan", swap)
-        probe_pieces = [probe_wave, got]
-        mine_amps = in_halves(by_slot(amplitudes[0], amplitudes[1]))
-        measured = brought(jnp.stack([mine_amps, got[:, size:]]), -ahead)
+        probe_pieces = [probe_wave, lax.ppermute(probe_wave, "scan", swap)]
+        straight = brought(by_slot(amplitudes[0], amplitudes[1]).astype(bf16), -ahead)
+        crossed = lax.ppermute(
+            by_slot(amplitudes[1], amplitudes[0]).astype(bf16),
+            ("tile", "scan"),
+            [((home - ahead) * 2 + x, home * 2 + 1 - x) for home in homes for x in range(2)],
+        )
+        measured = [straight, crossed]
     else:
         gathered = lax.all_gather(own, "scan")
         whole = jnp.stack([below(gathered[number]) for number in range(parts)])
         every = lax.all_gather(probe_wave, "scan")
         probe_pieces = [every[number] for number in range(parts)]
         every = lax.all_gather(brought(amplitudes.astype(bf16), -ahead), "scan")
-        measured = every[:, jnp.minimum(slot, slots - 1)].reshape((size, size))
+        measured = [every[:, jnp.minimum(slot, slots - 1)].reshape((size, size))]
     far_rows, far_cols, near = tables(size)
-    steps = range(-ahead, ahead + 1, 2)
-    arrived = {0: whole}
-    for step in sorted(steps, key=abs)[1:]:
-        arrived[step] = brought(whole, step)
-    notes = arrived[-ahead][0, -16, : slots + 1].astype(jnp.int32)
+    next_across, next_with = paired_across(whole, 4), paired_with(whole, 4)
+    near_across, near_with = paired_across(whole, 2), paired_with(whole, 2)
+    measured[0], next_across, next_with, near_across, near_with, probe_pieces = (
+        lax.optimization_barrier(
+            (measured[0], next_across, next_with, near_across, near_with, probe_pieces)
+        )
+    )
+    arrived = [
+        by_place(4, next_with, next_across),
+        by_place(2, near_with, near_across),
+        whole,
+        by_place(2, near_across, near_with),
+        by_place(4, next_across, next_with),
+    ]
+    notes = arrived[0][0, -16, : slots + 1].astype(jnp.int32)
     live = (slot < notes[slots]).astype(jnp.int32)
-    core = lax.rem(lax.axis_index("tile"), 2)
+    core = lax.rem(tile, 2)
     meta = jnp.stack(
         [notes[jnp.minimum(slot, slots - 1)], live, slot.astype(jnp.int32), core.astype(jnp.int32)]
     )
     turned, far_near, far_far = rolled(probe_pieces, far_rows, far_cols, meta, size)
-    mine = jnp.stack([arrived[step] for step in steps])
-    theirs = to_partner(mine)
+    mine = jnp.stack(arrived)
+    theirs = paired_with(mine, 1)
     shape = jax.ShapeDtypeStruct
     psi2, field = kernel_call(
         forth_kernel, size, tile_rows, "forth", 24 * size**3,
         [shape((2, size, size), bf16), shape((2, size, size), f32)],
         meta, mine, theirs, far_cols, near, turned, far_near,
     )
-    measured, field = lax.optimization_barrier((measured, field))
+    measured[-1], field = lax.optimization_barrier((measured[-1], field))
     amps = in_order(measured, slot.astype(jnp.int32)[None], size)
     keep, send = kernel_call(
         back_kernel, size, tile_rows, "back", 24 * size**3,
-        [shape((len(steps), parts, 2, 2, tile_rows, width), bf16)] * 2,
+        [shape((len(arrived), parts, 2, 2, tile_rows, width), bf16)] * 2,
         meta, mine, theirs, far_rows, near, turned, far_far, amps, psi2, field,
     )
-    merged = (keep.astype(f32) + to_partner(send).astype(f32)).astype(bf16)
+    merged = (keep.astype(f32) + paired_with(send, 1).astype(f32)).astype(bf16)
     total = sum(
-        (returned(merged[steps.index(step)], step) if step else merged[ahead // 2]).astype(f32)
-        for step in (2, -ahead, ahead, -2, 0)
+        value.astype(f32)
+        for value in (
+            paired_with(by_place(2, merged[1], merged[3]), 2),
+            paired_across(by_place(4, merged[4], merged[0]), 4),
+            paired_across(by_place(2, merged[3], merged[1]), 2),
+            paired_with(by_place(4, merged[0], merged[4]), 4),
+            merged[2],
+        )
     )
     if paired:
         away = lax.ppermute(by_slot(total[1], total[0]).astype(bf16), "scan", swap)

time: 86.5 us -> 79.7 us (0.921)
  the two profiles are of different devices: /device:TPU:0 before, /device:TPU:20 now
where the time goes in v1:
time: 79.7 us; the launch traced here: 79.2 us
  waiting for transfers between devices  28.8 us (36%)
  starting transfers between devices  21.7 us (27%)
  Pallas kernels  13.9 us (17%)
  other arithmetic  7.02 us (9%)
  local copies, waits for them, and re-layouts  6.05 us (8%)
  between operations  1.7 us (2%)
    ppermute x4, starting transfers between devices, paired_across(): return lax.ppermute(value, 'tile', pairs)  15.5 us
    ppermute x4, waiting for transfers between devices, paired_across(): return lax.ppermute(value, 'tile', pairs)  11.8 us
    pallas_call x2, Pallas kernels, kernel_call(): pl.pallas_call(functools.partial(kernel, size, size // tile_rows, tile_ro...  9.91 us
    ppermute x6, waiting for transfers between devices, paired_with(): lax.ppermute(value, 'tile', [(one, one ^ unit) for one in range(count)])  8.19 us
    unnamed x24, local copies, waits for them, and re-layouts  5.39 us
    ppermute x1, waiting for transfers between devices, shards(): away = lax.ppermute(by_slot(total[1], total[0]).astype(bf16), 'scan', swap)  4.95 us
    ppermute x1, waiting for transfers between devices, brought(): return lax.ppermute(value, 'tile', [(home + steps, home) for home in homes])  3.9 us
    pallas_call x1, Pallas kernels, rolled(): pl.pallas_call(functools.partial(roll_kernel, size), out_shape=[jax.Shape...  2.12 us
  transfers between devices with their start and end apart: 15, of which 9 were waited for; matrix products, arithmetic and copies ran while one was open for 5% of the time, Pallas kernels for 9%

profile of v1, /device:TPU:20, one launch (start us, length us, event | category | flops | bytes accessed | tf_op | source)
XLA Modules:
  0.0 79.2 jit_solution(5236610608135047545)
XLA Ops:
  0.0 1.0 %convert_element_type.68 = bf16[2,2,64,256]{3,2,1,0:T(8,128)(2,1)S(1)} convert(f32[2,2,64,256]{3,2,1,0:T(8,128)} %param.8) | non-fusion elementwise | flops 65536 | bytes 393216 | tf_op jit(solution)/shard_map/convert_element_type | solution.py:360
  1.1 1.6 %collective-permute-start.1 = (bf16[2,2,64,256]{3,2,1,0:T(8,128)(2,1)S(1)}, bf16[2,2,64,256]{3,2,1,0:T(8,128)(2,1)S(1)}, u32[]{:S(2)}, u32[]{:S(2)}) collective-permute-start(bf16[2,2,64,256]{3,2,1,0:T(8,128)(2,1)S(1)} %convert_element_type.68), channel_id=1, source_target_pairs={{0,1},{1,0},{2,3},{3,2},{4,5},{5,4},{6,7},{7,6},{8,9},{9,8},{10,11... | collective-permute-start | bytes 393224 | tf_op jit(solution)/shard_map/ppermute | solution.py:369
  2.6 2.0 %fusion.1 = (bf16[256,512]{1,0:T(8,128)(2,1)}, bf16[256,512]{1,0:T(8,128)(2,1)S(1)}) fusion(f32[2,256,512]{2,1,0:T(8,128)} %param.10, pred[]{:T(512)S(6)} %eq.15), kind=kLoop, calls=%fused_computation.12 | loop fusion | flops 262144 | bytes 1048577 | tf_op jit(solution)/shard_map/convert_element_type | solution.py:375
  4.6 1.3 %collective-permute-start = (bf16[256,512]{1,0:T(8,128)(2,1)S(1)}, bf16[256,512]{1,0:T(8,128)(2,1)S(1)}, u32[]{:S(2)}, u32[]{:S(2)}) collective-permute-start(bf16[256,512]{1,0:T(8,128)(2,1)S(1)} %get-tuple-element.44), channel_id=1, source_target_pairs={{0,8},{2,10},{4,12},{6,14},{8,16},{10,18},{12,20},{14,22},{1,9},{3... | collective-permute-start | bytes 786440 | tf_op jit(solution)/shard_map/ppermute | solution.py:340
  7.9 3.8 %collective-permute-start.4 = (bf16[2,272,256]{2,1,0:T(8,128)(2,1)S(1)}, bf16[2,272,256]{2,1,0:T(8,128)(2,1)S(1)}, u32[]{:S(2)}, u32[]{:S(2)}) collective-permute-start(bf16[2,272,256]{2,1,0:T(8,128)(2,1)S(1)} %pad_maximum_fusion), channel_id=1, source_target_pairs={{4,8},{6,10},{8,4},{10,6},{12,16},{14,18},{16,12},{18,14},{20,24},... | collective-permute-start | bytes 835592 | tf_op jit(solution)/shard_map/ppermute | solution.py:350
  11.8 3.9 %collective-permute-done.refs_0_ = bf16[256,512]{1,0:T(8,128)(2,1)S(1)} collective-permute-done((bf16[256,512]{1,0:T(8,128)(2,1)S(1)}, bf16[256,512]{1,0:T(8,128)(2,1)S(1)}, u32[]{:S(2)}, u32[]{:S(2)}) %collective-permute-start) | collective-permute-done | bytes 262176 | tf_op jit(solution)/shard_map/ppermute | solution.py:340
  15.7 0.7 copy-done.3
  16.4 1.9 %collective-permute-start.2 = (bf16[2,272,256]{2,1,0:T(8,128)(2,1)S(1)}, bf16[2,272,256]{2,1,0:T(8,128)(2,1)S(1)}, u32[]{:S(2)}, u32[]{:S(2)}) collective-permute-start(bf16[2,272,256]{2,1,0:T(8,128)(2,1)S(1)} %pad_maximum_fusion), channel_id=1, source_target_pairs={{8,16},{10,18},{12,20},{14,22},{16,8},{18,10},{20,12},{22,14},{9,1... | collective-permute-start | bytes 835592 | tf_op jit(solution)/shard_map/ppermute | solution.py:350
  18.4 2.8 %collective-permute-done.5 = bf16[2,272,256]{2,1,0:T(8,128)(2,1)S(1)} collective-permute-done((bf16[2,272,256]{2,1,0:T(8,128)(2,1)S(1)}, bf16[2,272,256]{2,1,0:T(8,128)(2,1)S(1)}, u32[]{:S(2)}, u32[]{:S(2)}) %collective-permute-start.5) | collective-permute-done | bytes 278560 | tf_op jit(solution)/shard_map/ppermute | solution.py:343
  21.2 1.6 %collective-permute-done.3 = bf16[2,272,256]{2,1,0:T(8,128)(2,1)S(1)} collective-permute-done((bf16[2,272,256]{2,1,0:T(8,128)(2,1)S(1)}, bf16[2,272,256]{2,1,0:T(8,128)(2,1)S(1)}, u32[]{:S(2)}, u32[]{:S(2)}) %collective-permute-start.3) | collective-permute-done | bytes 278560 | tf_op jit(solution)/shard_map/ppermute | solution.py:343
  22.8 3.4 %collective-permute-done.2 = bf16[2,272,256]{2,1,0:T(8,128)(2,1)S(1)} collective-permute-done((bf16[2,272,256]{2,1,0:T(8,128)(2,1)S(1)}, bf16[2,272,256]{2,1,0:T(8,128)(2,1)S(1)}, u32[]{:S(2)}, u32[]{:S(2)}) %collective-permute-start.2) | collective-permute-done | bytes 278560 | tf_op jit(solution)/shard_map/ppermute | solution.py:350
  26.2 0.8 copy-done.1
  26.9 0.8 bitcast_dynamic-update-slice_fusion.4
  28.0 1.3 %collective-permute-start.8 = (bf16[256,512]{1,0:T(8,128)(2,1)}, bf16[256,512]{1,0:T(8,128)(2,1)}, u32[]{:S(2)}, u32[]{:S(2)}) collective-permute-start(bf16[256,512]{1,0:T(8,128)(2,1)} %get-tuple-element.43), channel_id=1, source_target_pairs={{0,9},{1,8},{2,11},{3,10},{4,13},{5,12},{6,15},{7,14},{8,17},{9,16... | collective-permute-start | bytes 786440 | tf_op jit(solution)/shard_map/ppermute | solution.py:374
  29.3 0.7 slice_convert_fusion
  30.0 0.7 constant_dynamic-slice_fusion
  31.4 0.6 pad_add_fusion.meta
  32.0 1.0 %copy-done.2 = bf16[2,512,256]{2,1,0:T(8,128)(2,1)S(1)} copy-done((bf16[2,512,256]{2,1,0:T(8,128)(2,1)S(1)}, bf16[2,512,256]{2,1,0:T(8,128)(2,1)}, u32[]{:S(2)}) %copy-start.2) | copy-done | bytes 524312
  33.1 1.4 %copy-done.5 = bf16[3,512,512]{2,1,0:T(8,128)(2,1)S(1)} copy-done((bf16[3,512,512]{2,1,0:T(8,128)(2,1)S(1)}, bf16[3,512,512]{2,1,0:T(8,128)(2,1)}, u32[]{:S(2)}) %copy-start.5) | copy-done | bytes 1572888
  34.5 1.4 %copy-done.8 = bf16[3,512,512]{2,1,0:T(8,128)(2,1)S(1)} copy-done((bf16[3,512,512]{2,1,0:T(8,128)(2,1)S(1)}, bf16[3,512,512]{2,1,0:T(8,128)(2,1)}, u32[]{:S(2)}) %copy-start.8) | copy-done | bytes 1572888
  35.9 2.1 %rolled.1 = (bf16[2,512,512]{2,1,0:T(8,128)(2,1)S(1)}, bf16[3,512,256]{2,1,0:T(8,128)(2,1)S(1)}, bf16[3,256,512]{2,1,0:T(8,128)(2,1)S(1)}) custom-call(s32[4]{0:T(128)S(1)} %pad_add_fusion.meta, bf16[3,512,512]{2,1,0:T(8,128)(2,1)S(1)} %copy-done.5, bf16[3,512,512]{2,1,0:T(8,128)(2,1)S(1)} %copy-done.8, bf16[2,512,256]{2,1,0:T(8,128)(2,1)S(1)} %copy-done, ...), custom_call_target="tpu_custom_call" | custom-call | flops 8589934592 | bytes 6291456 | tf_op jit(solution)/shard_map/rolled/pallas_call | solution.py:129
  38.1 4.8 %forth.1 = (bf16[2,512,512]{2,1,0:T(8,128)(2,1)S(1)}, f32[2,512,512]{2,1,0:T(8,128)S(1)}) custom-call(s32[4]{0:T(128)S(1)} %pad_add_fusion.meta, bf16[5,2,272,256]{3,2,1,0:T(8,128)(2,1)S(1)} %bitcast_dynamic-update-slice_fusion.mine, bf16[5,2,272,256]{3,2,1,0:T(8,128)(2,1)S(1)} %collective-permute-done.7.theirs, bf16[3,512,512]{2,1,0:T(8,128)(2,1)S(1)} %copy-done.9, ...), custom_call_target="tpu_custom_call" | custom-call | flops 3221225472 | bytes 262144 | tf_op jit(solution)/shard_map/forth/pallas_call | solution.py:310
  42.9 1.9 %in_order.1.amps = bf16[512,512]{1,0:T(8,128)(2,1)S(1)} custom-call(s32[1]{0:T(128)} %bitcast.10.slot, bf16[256,512]{1,0:T(8,128)(2,1)S(1)} %copy-done.4, bf16[256,512]{1,0:T(8,128)(2,1)} %collective-permute-done.8.refs_1_), custom_call_target="tpu_custom_call" | custom-call | flops 536870912 | bytes 1048576 | tf_op jit(solution)/shard_map/in_order/pallas_call | solution.py:83
  44.8 5.1 %back.1 = (bf16[5,2,2,2,64,256]{5,4,3,2,1,0:T(8,128)(2,1)S(1)}, bf16[5,2,2,2,64,256]{5,4,3,2,1,0:T(8,128)(2,1)S(1)}) custom-call(s32[4]{0:T(128)S(1)} %pad_add_fusion.meta, bf16[5,2,272,256]{3,2,1,0:T(8,128)(2,1)S(1)} %bitcast_dynamic-update-slice_fusion.mine, bf16[5,2,272,256]{3,2,1,0:T(8,128)(2,1)S(1)} %collective-permute-done.7.theirs, ...), custom_call_target="tpu_custom_call" | custom-call | flops 3221225472 | bytes 262144 | tf_op jit(solution)/shard_map/back/pallas_call | solution.py:310
  50.5 2.7 %collective-permute-done.9 = bf16[5,2,2,2,64,256]{5,4,3,2,1,0:T(8,128)(2,1)S(1)} collective-permute-done((bf16[5,2,2,2,64,256]{5,4,3,2,1,0:T(8,128)(2,1)S(1)}, bf16[5,2,2,2,64,256]{5,4,3,2,1,0:T(8,128)(2,1)S(1)}, u32[]{:S(2)}, u32[]{:S(2)}) %collective-permute-start.9) | collective-permute-done | bytes 1310752 | tf_op jit(solution)/shard_map/ppermute | solution.py:343
  53.8 4.5 %collective-permute-start.11 = (bf16[2,2,2,64,256]{4,3,2,1,0:T(8,128)(2,1)S(1)}, bf16[2,2,2,64,256]{4,3,2,1,0:T(8,128)(2,1)S(1)}, u32[]{:S(2)}, u32[]{:S(2)}) collective-permute-start(bf16[2,2,2,64,256]{4,3,2,1,0:T(8,128)(2,1)S(1)} %get-tuple-element.40), channel_id=1, source_target_pairs={{8,16},{10,18},{12,20},{14,22},{16,8},{18,10},{20,12},{22,14},{9,1... | collective-permute-start | bytes 786440 | tf_op jit(solution)/shard_map/ppermute | solution.py:350
  58.3 5.3 %collective-permute-start.12 = (bf16[2,2,2,64,256]{4,3,2,1,0:T(8,128)(2,1)S(1)}, bf16[2,2,2,64,256]{4,3,2,1,0:T(8,128)(2,1)S(1)}, u32[]{:S(2)}, u32[]{:S(2)}) collective-permute-start(bf16[2,2,2,64,256]{4,3,2,1,0:T(8,128)(2,1)S(1)} %get-tuple-element.42), channel_id=1, source_target_pairs={{4,8},{6,10},{8,4},{10,6},{12,16},{14,18},{16,12},{18,14},{20,24},... | collective-permute-start | bytes 786440 | tf_op jit(solution)/shard_map/ppermute | solution.py:350
  63.7 1.6 %collective-permute-done.11 = bf16[2,2,2,64,256]{4,3,2,1,0:T(8,128)(2,1)S(1)} collective-permute-done((bf16[2,2,2,64,256]{4,3,2,1,0:T(8,128)(2,1)S(1)}, bf16[2,2,2,64,256]{4,3,2,1,0:T(8,128)(2,1)S(1)}, u32[]{:S(2)}, u32[]{:S(2)}) %collective-permute-start.11) | collective-permute-done | bytes 262176 | tf_op jit(solution)/shard_map/ppermute | solution.py:350
  65.3 1.1 %collective-permute-done.13 = bf16[2,2,2,64,256]{4,3,2,1,0:T(8,128)(2,1)S(1)} collective-permute-done((bf16[2,2,2,64,256]{4,3,2,1,0:T(8,128)(2,1)S(1)}, bf16[2,2,2,64,256]{4,3,2,1,0:T(8,128)(2,1)S(1)}, u32[]{:S(2)}, u32[]{:S(2)}) %collective-permute-start.13) | collective-permute-done | bytes 262176 | tf_op jit(solution)/shard_map/ppermute | solution.py:343
  66.5 6.8 %collective-permute-done.12 = bf16[2,2,2,64,256]{4,3,2,1,0:T(8,128)(2,1)S(1)} collective-permute-done((bf16[2,2,2,64,256]{4,3,2,1,0:T(8,128)(2,1)S(1)}, bf16[2,2,2,64,256]{4,3,2,1,0:T(8,128)(2,1)S(1)}, u32[]{:S(2)}, u32[]{:S(2)}) %collective-permute-start.12) | collective-permute-done | bytes 262176 | tf_op jit(solution)/shard_map/ppermute | solution.py:350
  73.5 5.0 %collective-permute-done.14 = bf16[2,2,64,256]{3,2,1,0:T(8,128)(2,1)S(1)} collective-permute-done((bf16[2,2,64,256]{3,2,1,0:T(8,128)(2,1)S(1)}, bf16[2,2,64,256]{3,2,1,0:T(8,128)(2,1)S(1)}, u32[]{:S(2)}, u32[]{:S(2)}) %collective-permute-start.14) | collective-permute-done | bytes 131104 | tf_op jit(solution)/shard_map/ppermute | solution.py:436
  78.5 0.8 bitcast_add_fusion
  (46 shorter events, 3.3 us)
Async XLA Ops:
  0.0 7.2 %copy-start.10 = (f32[2,2,64,256]{3,2,1,0:T(8,128)S(1)}, f32[2,2,64,256]{3,2,1,0:T(8,128)}, u32[]{:S(2)}) copy-start(f32[2,2,64,256]{3,2,1,0:T(8,128)} %param.8) | copy-start | bytes 786436
  0.0 5.9 %copy-start = (bf16[2,512,256]{2,1,0:T(8,128)(2,1)S(1)}, bf16[2,512,256]{2,1,0:T(8,128)(2,1)}, u32[]{:S(2)}) copy-start(bf16[2,512,256]{2,1,0:T(8,128)(2,1)} %refs_0_) | copy-start | bytes 1572868
  0.0 6.5 %copy-start.11 = (s32[2]{0:T(128)S(1)}, s32[2]{0:T(128)}, u32[]{:S(2)}) copy-start(s32[2]{0:T(128)} %param.11) | copy-start | bytes 28
  1.1 6.2 %collective-permute-start.1 = (bf16[2,2,64,256]{3,2,1,0:T(8,128)(2,1)S(1)}, bf16[2,2,64,256]{3,2,1,0:T(8,128)(2,1)S(1)}, u32[]{:S(2)}, u32[]{:S(2)}) collective-permute-start(bf16[2,2,64,256]{3,2,1,0:T(8,128)(2,1)S(1)} %convert_element_type.68), channel_id=1, source_target_pairs={{0,1},{1,0},{2,3},{3,2},{4,5},{5,4},{6,7},{7,6},{8,9},{9,8},{10,11... | collective-permute-start | bytes 393224 | tf_op jit(solution)/shard_map/ppermute | solution.py:369
  4.6 11.1 %collective-permute-start = (bf16[256,512]{1,0:T(8,128)(2,1)S(1)}, bf16[256,512]{1,0:T(8,128)(2,1)S(1)}, u32[]{:S(2)}, u32[]{:S(2)}) collective-permute-start(bf16[256,512]{1,0:T(8,128)(2,1)S(1)} %get-tuple-element.44), channel_id=1, source_target_pairs={{0,8},{2,10},{4,12},{6,14},{8,16},{10,18},{12,20},{14,22},{1,9},{3... | collective-permute-start | bytes 786440 | tf_op jit(solution)/shard_map/ppermute | solution.py:340
  5.9 20.3 %collective-permute-start.6 = (bf16[2,512,256]{2,1,0:T(8,128)(2,1)S(1)}, bf16[2,512,256]{2,1,0:T(8,128)(2,1)S(1)}, u32[]{:S(2)}, u32[]{:S(2)}) collective-permute-start(bf16[2,512,256]{2,1,0:T(8,128)(2,1)S(1)} %copy-done), channel_id=1, source_target_pairs={{0,1},{1,0},{2,3},{3,2},{4,5},{5,4},{6,7},{7,6},{8,9},{9,8},{10,11... | collective-permute-start | bytes 1572872 | tf_op jit(solution)/shard_map/ppermute | solution.py:372
  7.3 13.9 %collective-permute-start.5 = (bf16[2,272,256]{2,1,0:T(8,128)(2,1)S(1)}, bf16[2,272,256]{2,1,0:T(8,128)(2,1)S(1)}, u32[]{:S(2)}, u32[]{:S(2)}) collective-permute-start(bf16[2,272,256]{2,1,0:T(8,128)(2,1)S(1)} %pad_maximum_fusion), channel_id=1, source_target_pairs={{0,4},{2,6},{4,0},{6,2},{8,12},{10,14},{12,8},{14,10},{16,20},{18,... | collective-permute-start | bytes 835592 | tf_op jit(solution)/shard_map/ppermute | solution.py:343
  7.9 13.3 %collective-permute-start.4 = (bf16[2,272,256]{2,1,0:T(8,128)(2,1)S(1)}, bf16[2,272,256]{2,1,0:T(8,128)(2,1)S(1)}, u32[]{:S(2)}, u32[]{:S(2)}) collective-permute-start(bf16[2,272,256]{2,1,0:T(8,128)(2,1)S(1)} %pad_maximum_fusion), channel_id=1, source_target_pairs={{4,8},{6,10},{8,4},{10,6},{12,16},{14,18},{16,12},{18,14},{20,24},... | collective-permute-start | bytes 835592 | tf_op jit(solution)/shard_map/ppermute | solution.py:350
  11.7 11.1 %collective-permute-start.3 = (bf16[2,272,256]{2,1,0:T(8,128)(2,1)S(1)}, bf16[2,272,256]{2,1,0:T(8,128)(2,1)S(1)}, u32[]{:S(2)}, u32[]{:S(2)}) collective-permute-start(bf16[2,272,256]{2,1,0:T(8,128)(2,1)S(1)} %pad_maximum_fusion), channel_id=1, source_target_pairs={{0,8},{2,10},{4,12},{6,14},{8,0},{10,2},{12,4},{14,6},{16,24},{18,... | collective-permute-start | bytes 835592 | tf_op jit(solution)/shard_map/ppermute | solution.py:343
  15.7 0.7 copy-start.3
  16.4 9.8 %collective-permute-start.2 = (bf16[2,272,256]{2,1,0:T(8,128)(2,1)S(1)}, bf16[2,272,256]{2,1,0:T(8,128)(2,1)S(1)}, u32[]{:S(2)}, u32[]{:S(2)}) collective-permute-start(bf16[2,272,256]{2,1,0:T(8,128)(2,1)S(1)} %pad_maximum_fusion), channel_id=1, source_target_pairs={{8,16},{10,18},{12,20},{14,22},{16,8},{18,10},{20,12},{22,14},{9,1... | collective-permute-start | bytes 835592 | tf_op jit(solution)/shard_map/ppermute | solution.py:350
  26.2 0.8 copy-start.1
  28.0 10.1 %collective-permute-start.7 = (bf16[5,2,272,256]{3,2,1,0:T(8,128)(2,1)S(1)}, bf16[5,2,272,256]{3,2,1,0:T(8,128)(2,1)S(1)}, u32[]{:S(2)}, u32[]{:S(2)}) collective-permute-start(bf16[5,2,272,256]{3,2,1,0:T(8,128)(2,1)S(1)} %bitcast_dynamic-update-slice_fusion.mine), channel_id=1, source_target_pairs={{0,2},{2,0},{4,6},{6,4},{8,10},{10,8},{12,14},{14,12},{16,18},{18,... | collective-permute-start | bytes 4177928 | tf_op jit(solution)/shard_map/ppermute | solution.py:343
  28.0 14.9 %collective-permute-start.8 = (bf16[256,512]{1,0:T(8,128)(2,1)}, bf16[256,512]{1,0:T(8,128)(2,1)}, u32[]{:S(2)}, u32[]{:S(2)}) collective-permute-start(bf16[256,512]{1,0:T(8,128)(2,1)} %get-tuple-element.43), channel_id=1, source_target_pairs={{0,9},{1,8},{2,11},{3,10},{4,13},{5,12},{6,15},{7,14},{8,17},{9,16... | collective-permute-start | bytes 786440 | tf_op jit(solution)/shard_map/ppermute | solution.py:374
  32.0 1.0 %copy-start.2 = (bf16[2,512,256]{2,1,0:T(8,128)(2,1)S(1)}, bf16[2,512,256]{2,1,0:T(8,128)(2,1)}, u32[]{:S(2)}) copy-start(bf16[2,512,256]{2,1,0:T(8,128)(2,1)} %copy-done.1) | copy-start | bytes 1572868
  33.1 1.4 %copy-start.5 = (bf16[3,512,512]{2,1,0:T(8,128)(2,1)S(1)}, bf16[3,512,512]{2,1,0:T(8,128)(2,1)}, u32[]{:S(2)}) copy-start(bf16[3,512,512]{2,1,0:T(8,128)(2,1)} %constant.82.clone.far_rows) | copy-start | bytes 4718596
  34.5 1.4 %copy-start.8 = (bf16[3,512,512]{2,1,0:T(8,128)(2,1)S(1)}, bf16[3,512,512]{2,1,0:T(8,128)(2,1)}, u32[]{:S(2)}) copy-start(bf16[3,512,512]{2,1,0:T(8,128)(2,1)} %constant.83.clone.far_cols) | copy-start | bytes 4718596
  35.9 2.1 %copy-start.7 = (bf16[3,512,512]{2,1,0:T(8,128)(2,1)S(1)}, bf16[3,512,512]{2,1,0:T(8,128)(2,1)}, u32[]{:S(2)}) copy-start(bf16[3,512,512]{2,1,0:T(8,128)(2,1)} %constant.84.clone.near) | copy-start | bytes 4718596
  35.9 2.2 %copy-start.9 = (bf16[3,512,512]{2,1,0:T(8,128)(2,1)S(1)}, bf16[3,512,512]{2,1,0:T(8,128)(2,1)}, u32[]{:S(2)}) copy-start(bf16[3,512,512]{2,1,0:T(8,128)(2,1)} %constant.83.clone.far_cols) | copy-start | bytes 4718596
  38.1 4.9 %copy-start.4 = (bf16[256,512]{1,0:T(8,128)(2,1)S(1)}, bf16[256,512]{1,0:T(8,128)(2,1)}, u32[]{:S(2)}) copy-start(bf16[256,512]{1,0:T(8,128)(2,1)} %copy-done.3) | copy-start | bytes 786436
  42.9 1.9 %copy-start.6 = (bf16[3,512,512]{2,1,0:T(8,128)(2,1)S(1)}, bf16[3,512,512]{2,1,0:T(8,128)(2,1)}, u32[]{:S(2)}) copy-start(bf16[3,512,512]{2,1,0:T(8,128)(2,1)} %constant.82.clone.far_rows) | copy-start | bytes 4718596
  49.9 3.2 %collective-permute-start.9 = (bf16[5,2,2,2,64,256]{5,4,3,2,1,0:T(8,128)(2,1)S(1)}, bf16[5,2,2,2,64,256]{5,4,3,2,1,0:T(8,128)(2,1)S(1)}, u32[]{:S(2)}, u32[]{:S(2)}) collective-permute-start(bf16[5,2,2,2,64,256]{5,4,3,2,1,0:T(8,128)(2,1)S(1)} %get-tuple-element.36), channel_id=1, source_target_pairs={{0,2},{2,0},{4,6},{6,4},{8,10},{10,8},{12,14},{14,12},{16,18},{18,... | collective-permute-start | bytes 3932168 | tf_op jit(solution)/shard_map/ppermute | solution.py:343
  53.7 10.0 %collective-permute-start.10 = (bf16[2,2,2,64,256]{4,3,2,1,0:T(8,128)(2,1)S(1)}, bf16[2,2,2,64,256]{4,3,2,1,0:T(8,128)(2,1)S(1)}, u32[]{:S(2)}, u32[]{:S(2)}) collective-permute-start(bf16[2,2,2,64,256]{4,3,2,1,0:T(8,128)(2,1)S(1)} %get-tuple-element.39), channel_id=1, source_target_pairs={{0,4},{2,6},{4,0},{6,2},{8,12},{10,14},{12,8},{14,10},{16,20},{18,... | collective-permute-start | bytes 786440 | tf_op jit(solution)/shard_map/ppermute | solution.py:343
  53.8 11.5 %collective-permute-start.11 = (bf16[2,2,2,64,256]{4,3,2,1,0:T(8,128)(2,1)S(1)}, bf16[2,2,2,64,256]{4,3,2,1,0:T(8,128)(2,1)S(1)}, u32[]{:S(2)}, u32[]{:S(2)}) collective-permute-start(bf16[2,2,2,64,256]{4,3,2,1,0:T(8,128)(2,1)S(1)} %get-tuple-element.40), channel_id=1, source_target_pairs={{8,16},{10,18},{12,20},{14,22},{16,8},{18,10},{20,12},{22,14},{9,1... | collective-permute-start | bytes 786440 | tf_op jit(solution)/shard_map/ppermute | solution.py:350
  58.3 8.2 %collective-permute-start.13 = (bf16[2,2,2,64,256]{4,3,2,1,0:T(8,128)(2,1)S(1)}, bf16[2,2,2,64,256]{4,3,2,1,0:T(8,128)(2,1)S(1)}, u32[]{:S(2)}, u32[]{:S(2)}) collective-permute-start(bf16[2,2,2,64,256]{4,3,2,1,0:T(8,128)(2,1)S(1)} %get-tuple-element.41), channel_id=1, source_target_pairs={{0,8},{2,10},{4,12},{6,14},{8,0},{10,2},{12,4},{14,6},{16,24},{18,... | collective-permute-start | bytes 786440 | tf_op jit(solution)/shard_map/ppermute | solution.py:343
  58.3 14.9 %collective-permute-start.12 = (bf16[2,2,2,64,256]{4,3,2,1,0:T(8,128)(2,1)S(1)}, bf16[2,2,2,64,256]{4,3,2,1,0:T(8,128)(2,1)S(1)}, u32[]{:S(2)}, u32[]{:S(2)}) collective-permute-start(bf16[2,2,2,64,256]{4,3,2,1,0:T(8,128)(2,1)S(1)} %get-tuple-element.42), channel_id=1, source_target_pairs={{4,8},{6,10},{8,4},{10,6},{12,16},{14,18},{16,12},{18,14},{20,24},... | collective-permute-start | bytes 786440 | tf_op jit(solution)/shard_map/ppermute | solution.py:350
  73.4 5.0 %collective-permute-start.14 = (bf16[2,2,64,256]{3,2,1,0:T(8,128)(2,1)S(1)}, bf16[2,2,64,256]{3,2,1,0:T(8,128)(2,1)S(1)}, u32[]{:S(2)}, u32[]{:S(2)}) collective-permute-start(bf16[2,2,64,256]{3,2,1,0:T(8,128)(2,1)S(1)} %fusion.4), channel_id=1, source_target_pairs={{0,1},{1,0},{2,3},{3,2},{4,5},{5,4},{6,7},{7,6},{8,9},{9,8},{10,11... | collective-permute-start | bytes 393224 | tf_op jit(solution)/shard_map/ppermute | solution.py:436

commit v2 on v1

--- a/solution.py
+++ b/solution.py
@@ -26,15 +26,20 @@
     near = (base * kernel[None, :]) @ np.conj(base).T / size
 
     def parts(table):
-        stacked = np.stack([table.real, table.imag, -table.imag])
+        stacked = np.stack([table.real, table.imag])
         return jnp.asarray(stacked.astype(ml_dtypes.bfloat16))
 
     order = np.concatenate([index[0::2], index[1::2]])
     return parts(far[order]), parts(far[:, order]), parts(near)
 
 
+def three(table, conjugate):
+    real, imag = table
+    return (real, -imag, imag) if conjugate else (real, imag, -imag)
+
+
 def left(table, conjugate, wave):
-    real, plus, minus = table if not conjugate else (table[0], table[2], table[1])
+    real, plus, minus = three(table, conjugate)
     top = jnp.concatenate([real, minus], axis=1)
     bottom = jnp.concatenate([plus, real], axis=1)
     return (
@@ -44,7 +49,7 @@
 
 
 def right(table, conjugate, wave):
-    real, plus, minus = table if not conjugate else (table[0], table[2], table[1])
+    real, plus, minus = three(table, conjugate)
     real_side = jnp.concatenate([real, minus], axis=0)
     imag_side = jnp.concatenate([plus, real], axis=0)
     return (
@@ -59,39 +64,22 @@
     return jnp.where(hit(row, col), 1.0, 0.0).astype(bf16)
 
 
-def order_kernel(size, slot, *refs):
-    measured, (ordered, amps) = refs[:-2], refs[-2:]
+def in_order(size, slot, measured, amps):
     half = size // 2
     for number, piece in enumerate(measured):
-        rows = piece.shape[0]
-        at = pl.multiple_of(jnp.where(slot[0] == number, 0, size - rows), rows)
-        amps[pl.ds(at, rows), :] = piece[...]
+        rows = size // len(measured)
+        at = pl.multiple_of(jnp.where(slot == number, 0, size - rows), rows)
+        amps[pl.ds(at, rows), :] = piece[0:rows, :]
 
     def frequency(place, natural):
         return natural == jnp.where(place < half, 2 * place, 2 * (place - half) + 1)
 
     rows_first = jnp.dot(one_hot(size, frequency), amps[...], preferred_element_type=f32)
-    ordered[...] = jnp.dot(
+    return jnp.dot(
         rows_first.astype(bf16),
         one_hot(size, lambda row, col: frequency(col, row)),
         preferred_element_type=f32,
-    ).astype(bf16)
-
-
-def in_order(measured, slot, size):
-    whole = pl.BlockSpec(memory_space=pltpu.VMEM)
-    return pl.pallas_call(
-        functools.partial(order_kernel, size),
-        out_shape=jax.ShapeDtypeStruct((size, size), bf16),
-        in_specs=[pl.BlockSpec(memory_space=pltpu.SMEM)] + [whole] * len(measured),
-        out_specs=whole,
-        scratch_shapes=[pltpu.VMEM((size, size), bf16)],
-        compiler_params=pltpu.CompilerParams(vmem_limit_bytes=16 * 1024 * 1024),
-        cost_estimate=pl.CostEstimate(
-            flops=4 * size**3, bytes_accessed=4 * size * size, transcendentals=0
-        ),
-        name="in_order",
-    )(slot, *measured)
+    )
 
 
 def roll_kernel(size, meta, far_rows, far_cols, *refs):
@@ -105,7 +93,7 @@
 
     down = one_hot(size, moved)
     across = one_hot(size, lambda row, col: moved(col, row))
-    for c in range(3):
+    for c in range(2):
         near_side[c] = jnp.dot(
             far_rows[c], across[:, :half], preferred_element_type=f32
         ).astype(bf16)
@@ -130,12 +118,12 @@
         functools.partial(roll_kernel, size),
         out_shape=[
             jax.ShapeDtypeStruct((2, size, size), bf16),
-            jax.ShapeDtypeStruct((3, size, size // 2), bf16),
-            jax.ShapeDtypeStruct((3, size // 2, size), bf16),
+            jax.ShapeDtypeStruct((2, size, size // 2), bf16),
+            jax.ShapeDtypeStruct((2, size // 2, size), bf16),
         ],
         in_specs=[pl.BlockSpec(memory_space=pltpu.SMEM)] + [whole] * (2 + len(pieces)),
         out_specs=[whole] * 3,
-        compiler_params=pltpu.CompilerParams(vmem_limit_bytes=24 * 1024 * 1024),
+        compiler_params=pltpu.CompilerParams(vmem_limit_bytes=16 * 1024 * 1024),
         cost_estimate=pl.CostEstimate(
             flops=64 * size**3, bytes_accessed=24 * size * size, transcendentals=0
         ),
@@ -145,7 +133,7 @@
 
 def tile_access(size, span, tile_rows, meta, mine, theirs):
     offset, core = meta[0], meta[3]
-    parts, _, width = mine.shape[1:]
+    parts, _, _, _, width = mine.shape[1:]
     early = lax.broadcasted_iota(jnp.int32, (tile_rows, width), 0) < offset
 
     def place(k):
@@ -153,8 +141,7 @@
 
     def piece(k, h, s, c):
         source = mine if k % 2 == 0 else theirs
-        at = (2 * s + c) * tile_rows
-        return source[place(k), h, at : at + tile_rows, :].astype(f32)
+        return source[place(k), h, s, c].astype(f32)
 
     def patch(s, c):
         rows = []
@@ -197,7 +184,7 @@
 
 
 def parts_of(ref, rows, cols):
-    return ref[0, rows, cols], ref[1, rows, cols], ref[2, rows, cols]
+    return ref[0, rows, cols], ref[1, rows, cols]
 
 
 def both(first, second, axis):
@@ -249,9 +236,9 @@
 
 
 def back_kernel(
-    size, span, tile_rows, meta, mine, theirs, far_rows, near, probe, far_far, amps, psi2, field,
-    keep, send, rows_buf, cols_buf,
+    size, span, tile_rows, meta, mine, theirs, far_rows, near, probe, far_far, psi2, field, *refs,
 ):
+    measured, (keep, send, rows_buf, cols_buf) = refs[:-4], refs[-4:]
     core = meta[3]
     parts, _, _, _, width = keep.shape[1:]
     half = size // 2
@@ -273,10 +260,11 @@
                     target = keep if k % 2 == 0 else send
                     target[place(k), h, s, c] = block.astype(bf16)
 
+        amps = in_order(size, meta[2], measured, cols_buf.at[:, 0:size])
         chis = []
         for cols in (low, high):
             fr, fi = field[0, :, cols], field[1, :, cols]
-            keeping = 1.0 - amps[:, cols].astype(f32) * lax.rsqrt(fr * fr + fi * fi + smooth)
+            keeping = 1.0 - amps[:, cols] * lax.rsqrt(fr * fr + fi * fi + smooth)
             chis.append((fr * keeping, fi * keeping))
         put_col_halves(cols_buf, *chis)
         even = right(parts_of(far_rows, low, low), True, cols_buf[:, 0:size])
@@ -316,7 +304,7 @@
             pltpu.VMEM((2 * size, size), bf16),
             pltpu.VMEM((size, 2 * size), bf16),
         ],
-        compiler_params=pltpu.CompilerParams(vmem_limit_bytes=36 * 1024 * 1024),
+        compiler_params=pltpu.CompilerParams(vmem_limit_bytes=28 * 1024 * 1024),
         cost_estimate=pl.CostEstimate(
             flops=flops, bytes_accessed=size * size, transcendentals=0
         ),
@@ -333,20 +321,20 @@
     paired = parts == slots == 2
     slot = lax.axis_index("scan")
     ahead = span // 2
-    homes = range(ahead, count - ahead)
     swap = [(0, 1), (1, 0)]
-
-    def brought(value, steps):
-        return lax.ppermute(value, "tile", [(home + steps, home) for home in homes])
+    ahead_pairs = [(one, (one + ahead) % count) for one in range(count)]
+
+    def brought(value):
+        return lax.ppermute(value, "tile", ahead_pairs)
 
     def paired_with(value, unit):
         return lax.ppermute(value, "tile", [(one, one ^ unit) for one in range(count)])
 
     def paired_across(value, unit):
         pairs = []
-        for one in range(unit, count - unit):
+        for one in range(count):
             step = unit if (one // unit) % 2 else -unit
-            pairs.append((one, one + step))
+            pairs.append((one, one + step if unit <= one < count - unit else one))
         return lax.ppermute(value, "tile", pairs)
 
     def by_slot(first, second):
@@ -360,52 +348,47 @@
     own = object_slab.astype(bf16)
     width = own.shape[-1]
     notes = jnp.concatenate([row_offsets, position_counts]).astype(bf16)
-    notes = jnp.pad(notes[None], ((0, 15), (0, width - slots - 1)))
-
-    def below(tile):
-        return jnp.concatenate([tile.reshape((-1, width)), notes])
-
+    notes = jnp.pad(notes[None], ((0, 15), (0, size - slots - 1)))
     if paired:
         beside = lax.ppermute(own, "scan", swap)
-        whole = jnp.stack([below(by_slot(own, beside)), below(by_slot(beside, own))])
+        whole = jnp.stack([by_slot(own, beside), by_slot(beside, own)])
 
         probe_pieces = [probe_wave, lax.ppermute(probe_wave, "scan", swap)]
-        straight = brought(by_slot(amplitudes[0], amplitudes[1]).astype(bf16), -ahead)
+        straight, crossed = (by_slot(amplitudes[a], amplitudes[1 - a]).astype(bf16) for a in (0, 1))
+        straight = brought(jnp.concatenate([straight, notes]))
         crossed = lax.ppermute(
-            by_slot(amplitudes[1], amplitudes[0]).astype(bf16),
+            crossed,
             ("tile", "scan"),
-            [((home - ahead) * 2 + x, home * 2 + 1 - x) for home in homes for x in range(2)],
+            [(2 * a + x, 2 * b + 1 - x) for a, b in ahead_pairs for x in range(2)],
         )
+        notes = straight[-16]
         measured = [straight, crossed]
     else:
-        gathered = lax.all_gather(own, "scan")
-        whole = jnp.stack([below(gathered[number]) for number in range(parts)])
+        whole = lax.all_gather(own, "scan")
         every = lax.all_gather(probe_wave, "scan")
         probe_pieces = [every[number] for number in range(parts)]
-        every = lax.all_gather(brought(amplitudes.astype(bf16), -ahead), "scan")
+        notes = brought(notes)[0]
+        every = lax.all_gather(brought(amplitudes.astype(bf16)), "scan")
         measured = [every[:, jnp.minimum(slot, slots - 1)].reshape((size, size))]
     far_rows, far_cols, near = tables(size)
+    core = lax.rem(tile, 2)
+    notes = notes[: slots + 1].astype(jnp.int32)
+    home = (tile >= ahead) & (tile < count - ahead)
+    live = (home & (slot < notes[slots])).astype(jnp.int32)
+    meta = jnp.stack(
+        [notes[jnp.minimum(slot, slots - 1)], live, slot.astype(jnp.int32), core.astype(jnp.int32)]
+    )
+    turned, far_near, far_far = rolled(probe_pieces, far_rows, far_cols, meta, size)
     next_across, next_with = paired_across(whole, 4), paired_with(whole, 4)
     near_across, near_with = paired_across(whole, 2), paired_with(whole, 2)
-    measured[0], next_across, next_with, near_across, near_with, probe_pieces = (
-        lax.optimization_barrier(
-            (measured[0], next_across, next_with, near_across, near_with, probe_pieces)
-        )
-    )
+    middle, turned = lax.optimization_barrier((whole, turned))
     arrived = [
         by_place(4, next_with, next_across),
         by_place(2, near_with, near_across),
-        whole,
+        middle,
         by_place(2, near_across, near_with),
         by_place(4, next_across, next_with),
     ]
-    notes = arrived[0][0, -16, : slots + 1].astype(jnp.int32)
-    live = (slot < notes[slots]).astype(jnp.int32)
-    core = lax.rem(tile, 2)
-    meta = jnp.stack(
-        [notes[jnp.minimum(slot, slots - 1)], live, slot.astype(jnp.int32), core.astype(jnp.int32)]
-    )
-    turned, far_near, far_far = rolled(probe_pieces, far_rows, far_cols, meta, size)
     mine = jnp.stack(arrived)
     theirs = paired_with(mine, 1)
     shape = jax.ShapeDtypeStruct
@@ -415,20 +398,19 @@
         meta, mine, theirs, far_cols, near, turned, far_near,
     )
     measured[-1], field = lax.optimization_barrier((measured[-1], field))
-    amps = in_order(measured, slot.astype(jnp.int32)[None], size)
     keep, send = kernel_call(
         back_kernel, size, tile_rows, "back", 24 * size**3,
         [shape((len(arrived), parts, 2, 2, tile_rows, width), bf16)] * 2,
-        meta, mine, theirs, far_rows, near, turned, far_far, amps, psi2, field,
+        meta, mine, theirs, far_rows, near, turned, far_far, psi2, field, *measured,
     )
     merged = (keep.astype(f32) + paired_with(send, 1).astype(f32)).astype(bf16)
     total = sum(
         value.astype(f32)
         for value in (
+            paired_with(by_place(4, merged[0], merged[4]), 4),
+            paired_across(by_place(4, merged[4], merged[0]), 4),
             paired_with(by_place(2, merged[1], merged[3]), 2),
-            paired_across(by_place(4, merged[4], merged[0]), 4),
             paired_across(by_place(2, merged[3], merged[1]), 2),
-            paired_with(by_place(4, merged[0], merged[4]), 4),
             merged[2],
         )
     )

time: 79.7 us -> 77.7 us (0.975)
  the two profiles are of different devices: /device:TPU:20 before, /device:TPU:8 now
where the time goes in v2:
time: 77.7 us; the launch traced here: 77.1 us
  waiting for transfers between devices  24.9 us (32%)
  starting transfers between devices  23.4 us (30%)
  Pallas kernels  12.8 us (16%)
  other arithmetic  12.6 us (16%)
  local copies, waits for them, and re-layouts  1.77 us (2%)
  between operations  1.58 us (2%)
    ppermute x4, starting transfers between devices, paired_across(): return lax.ppermute(value, 'tile', pairs)  11.9 us
    pallas_call x2, Pallas kernels, kernel_call(): pl.pallas_call(functools.partial(kernel, size, size // tile_rows, tile_ro...  10.9 us
    ppermute x4, waiting for transfers between devices, paired_across(): return lax.ppermute(value, 'tile', pairs)  10.3 us
    ppermute x6, waiting for transfers between devices, paired_with(): lax.ppermute(value, 'tile', [(one, one ^ unit) for one in range(count)])  8.83 us
    ppermute x6, starting transfers between devices, paired_with(): lax.ppermute(value, 'tile', [(one, one ^ unit) for one in range(count)])  4.72 us
    ppermute x1, waiting for transfers between devices, shards(): away = lax.ppermute(by_slot(total[1], total[0]).astype(bf16), 'scan', swap)  3.98 us
    unnamed x3, other arithmetic  3.08 us
    ppermute x1, starting transfers between devices, shards(): lax.ppermute(crossed, ('tile', 'scan'), [(2 * a + x, 2 * b + 1 - x) for a...  2.06 us
  transfers between devices with their start and end apart: 15, of which 9 were waited for; matrix products, arithmetic and copies ran while one was open for 11% of the time, Pallas kernels for 6%

profile of v2, /device:TPU:8, one launch (start us, length us, event | category | flops | bytes accessed | tf_op | source)
XLA Modules:
  0.0 77.1 jit_solution(9008008277337286475)
XLA Ops:
  0.0 1.0 %convert_element_type.69 = bf16[2,2,64,256]{3,2,1,0:T(8,128)(2,1)S(1)} convert(f32[2,2,64,256]{3,2,1,0:T(8,128)} %param.8) | non-fusion elementwise | flops 65536 | bytes 393216 | tf_op jit(solution)/shard_map/convert_element_type | solution.py:348
  1.0 1.6 %collective-permute-start.1 = (bf16[2,2,64,256]{3,2,1,0:T(8,128)(2,1)S(1)}, bf16[2,2,64,256]{3,2,1,0:T(8,128)(2,1)}, u32[]{:S(2)}, u32[]{:S(2)}) collective-permute-start(bf16[2,2,64,256]{3,2,1,0:T(8,128)(2,1)S(1)} %convert_element_type.69), channel_id=1, source_target_pairs={{0,1},{1,0},{2,3},{3,2},{4,5},{5,4},{6,7},{7,6},{8,9},{9,8},{10,11... | collective-permute-start | bytes 393224 | tf_op jit(solution)/shard_map/ppermute | solution.py:353
  3.9 2.0 %fusion.1 = (bf16[256,512]{1,0:T(8,128)(2,1)}, bf16[256,512]{1,0:T(8,128)(2,1)S(1)}) fusion(f32[2,256,512]{2,1,0:T(8,128)} %param.10, pred[]{:T(512)S(6)} %eq.15), kind=kLoop, calls=%fused_computation.6 | loop fusion | flops 262144 | bytes 1048577 | tf_op jit(solution)/shard_map/convert_element_type | solution.py:357
  6.7 1.6 %collective-permute-start = (bf16[272,512]{1,0:T(8,128)(2,1)}, bf16[272,512]{1,0:T(8,128)(2,1)S(1)}, u32[]{:S(2)}, u32[]{:S(2)}) collective-permute-start(bf16[272,512]{1,0:T(8,128)(2,1)} %pad_maximum_fusion), channel_id=1, source_target_pairs={{0,8},{2,10},{4,12},{6,14},{8,16},{10,18},{12,20},{14,22},{16,24},... | collective-permute-start | bytes 835592 | tf_op jit(solution)/shard_map/ppermute | solution.py:328
  8.8 1.2 %select_bitcast_fusion.5 = (bf16[1,2,2,64,256]{4,3,2,1,0:T(8,128)(2,1)S(1)}, bf16[1,2,2,64,256]{4,3,2,1,0:T(8,128)(2,1)S(1)}) fusion(bf16[2,2,64,256]{3,2,1,0:T(8,128)(2,1)} %collective-permute-done.1, pred[]{:T(512)S(6)} %eq.15, f32[2,2,64,256]{3,2,1,0:T(8,128)} %param.8), kind=kLoop, calls=%fused_computation.22 | loop fusion | flops 196608 | bytes 655361 | tf_op jit(solution)/shard_map/stack | solution.py:354
  10.7 3.3 %collective-permute-start.5 = (bf16[2,2,2,64,256]{4,3,2,1,0:T(8,128)(2,1)}, bf16[2,2,2,64,256]{4,3,2,1,0:T(8,128)(2,1)}, u32[]{:S(2)}, u32[]{:S(2)}) collective-permute-start(bf16[2,2,2,64,256]{4,3,2,1,0:T(8,128)(2,1)} %pad_maximum_fusion.1), channel_id=1, source_target_pairs={{0,0},{2,2},{4,8},{6,10},{8,4},{10,6},{12,16},{14,18},{16,12},{18,... | collective-permute-start | bytes 786440 | tf_op jit(solution)/shard_map/ppermute | solution.py:338
  14.0 1.7 %collective-permute-start.4 = (bf16[2,2,2,64,256]{4,3,2,1,0:T(8,128)(2,1)}, bf16[2,2,2,64,256]{4,3,2,1,0:T(8,128)(2,1)}, u32[]{:S(2)}, u32[]{:S(2)}) collective-permute-start(bf16[2,2,2,64,256]{4,3,2,1,0:T(8,128)(2,1)} %pad_maximum_fusion.1), channel_id=1, source_target_pairs={{0,4},{2,6},{4,0},{6,2},{8,12},{10,14},{12,8},{14,10},{16,20},{18,... | collective-permute-start | bytes 786440 | tf_op jit(solution)/shard_map/ppermute | solution.py:331
  15.7 2.0 %collective-permute-start.3 = (bf16[2,2,2,64,256]{4,3,2,1,0:T(8,128)(2,1)}, bf16[2,2,2,64,256]{4,3,2,1,0:T(8,128)(2,1)}, u32[]{:S(2)}, u32[]{:S(2)}) collective-permute-start(bf16[2,2,2,64,256]{4,3,2,1,0:T(8,128)(2,1)} %pad_maximum_fusion.1), channel_id=1, source_target_pairs={{0,0},{2,2},{4,4},{6,6},{8,16},{10,18},{12,20},{14,22},{16,8},{18,... | collective-permute-start | bytes 786440 | tf_op jit(solution)/shard_map/ppermute | solution.py:338
  17.7 2.1 %collective-permute-start.2 = (bf16[2,2,2,64,256]{4,3,2,1,0:T(8,128)(2,1)}, bf16[2,2,2,64,256]{4,3,2,1,0:T(8,128)(2,1)}, u32[]{:S(2)}, u32[]{:S(2)}) collective-permute-start(bf16[2,2,2,64,256]{4,3,2,1,0:T(8,128)(2,1)} %pad_maximum_fusion.1), channel_id=1, source_target_pairs={{0,8},{2,10},{4,12},{6,14},{8,0},{10,2},{12,4},{14,6},{16,24},{18,... | collective-permute-start | bytes 786440 | tf_op jit(solution)/shard_map/ppermute | solution.py:331
  21.8 5.4 %collective-permute-done.3 = bf16[2,2,2,64,256]{4,3,2,1,0:T(8,128)(2,1)} collective-permute-done((bf16[2,2,2,64,256]{4,3,2,1,0:T(8,128)(2,1)}, bf16[2,2,2,64,256]{4,3,2,1,0:T(8,128)(2,1)}, u32[]{:S(2)}, u32[]{:S(2)}) %collective-permute-start.3) | collective-permute-done | bytes 262176 | tf_op jit(solution)/shard_map/ppermute | solution.py:338
  27.2 1.0 %bitcast_dynamic-update-slice_fusion.4 = bf16[5,2,2,2,64,256]{5,4,3,2,1,0:T(8,128)(2,1)S(1)} fusion(bf16[2,2,2,64,256]{4,3,2,1,0:T(8,128)(2,1)} %collective-permute-done.2, bf16[2,2,2,64,256]{4,3,2,1,0:T(8,128)(2,1)} %collective-permute-done.3, pred[]{:T(512)S(6)} %eq.30), kind=kLoop, calls=%fused_computation.14 | loop fusion | flops 131071 | bytes 786433
  28.3 1.0 %bitcast_dynamic-update-slice_fusion.3 = bf16[5,2,2,2,64,256]{5,4,3,2,1,0:T(8,128)(2,1)S(1)} fusion(bf16[5,2,2,2,64,256]{5,4,3,2,1,0:T(8,128)(2,1)S(1)} %bitcast_dynamic-update-slice_fusion.4, bf16[2,2,2,64,256]{4,3,2,1,0:T(8,128)(2,1)} %collective-permute-done.4, bf16[2,2,2,64,256]{4,3,2,1,0:T(8,128)(2,1)} %collective-permute-done.5, pred[]{:T(512)S(6)} %eq.31), kind=kLoop, calls=%fused_computation.13 | loop fusion | flops 131072 | bytes 786433
  29.3 1.9 %rolled.1 = (bf16[2,512,512]{2,1,0:T(8,128)(2,1)S(1)}, bf16[2,512,256]{2,1,0:T(8,128)(2,1)S(1)}, bf16[2,256,512]{2,1,0:T(8,128)(2,1)S(1)}) custom-call(s32[4]{0:T(128)S(1)} %pad_add_fusion.meta, bf16[2,512,512]{2,1,0:T(8,128)(2,1)S(1)} %copy-done.1, bf16[2,512,512]{2,1,0:T(8,128)(2,1)S(1)} %copy-done.3, bf16[2,512,256]{2,1,0:T(8,128)(2,1)S(1)} %copy-done, ...), custom_call_target="tpu_custom_call" | custom-call | flops 8589934592 | bytes 6291456 | tf_op jit(solution)/shard_map/rolled/pallas_call | solution.py:117
  31.2 1.1 %bitcast_dynamic-update-slice_fusion.2 = bf16[5,2,2,2,64,256]{5,4,3,2,1,0:T(8,128)(2,1)S(1)} fusion(bf16[5,2,2,2,64,256]{5,4,3,2,1,0:T(8,128)(2,1)S(1)} %bitcast_dynamic-update-slice_fusion.3, bf16[2,2,2,64,256]{4,3,2,1,0:T(8,128)(2,1)} %pad_maximum_fusion.1), kind=kLoop, calls=%fused_computation.12 | loop fusion | bytes 524288
  32.3 1.0 %bitcast_dynamic-update-slice_fusion.1 = bf16[5,2,2,2,64,256]{5,4,3,2,1,0:T(8,128)(2,1)S(1)} fusion(bf16[5,2,2,2,64,256]{5,4,3,2,1,0:T(8,128)(2,1)S(1)} %bitcast_dynamic-update-slice_fusion.2, bf16[2,2,2,64,256]{4,3,2,1,0:T(8,128)(2,1)} %collective-permute-done.5, bf16[2,2,2,64,256]{4,3,2,1,0:T(8,128)(2,1)} %collective-permute-done.4, pred[]{:T(512)S(6)} %eq.31), kind=kLoop, calls=%fused_computation.11 | loop fusion | flops 131072 | bytes 786433
  33.3 1.0 %bitcast_dynamic-update-slice_fusion.mine = bf16[5,2,2,2,64,256]{5,4,3,2,1,0:T(8,128)(2,1)S(1)} fusion(bf16[5,2,2,2,64,256]{5,4,3,2,1,0:T(8,128)(2,1)S(1)} %bitcast_dynamic-update-slice_fusion.1, bf16[2,2,2,64,256]{4,3,2,1,0:T(8,128)(2,1)} %collective-permute-done.3, bf16[2,2,2,64,256]{4,3,2,1,0:T(8,128)(2,1)} %collective-permute-done.2, pred[]{:T(512)S(6)} %eq.30), kind=kLoop, calls=%fused_computation.10 | loop fusion | flops 131072 | bytes 786433 | tf_op jit(solution)/shard_map/stack | solution.py:392
  34.4 2.1 %collective-permute-start.8 = (bf16[256,512]{1,0:T(8,128)(2,1)S(1)}, bf16[256,512]{1,0:T(8,128)(2,1)S(1)}, u32[]{:S(2)}, u32[]{:S(2)}) collective-permute-start(bf16[256,512]{1,0:T(8,128)(2,1)S(1)} %copy-done.4), channel_id=1, source_target_pairs={{0,9},{1,8},{2,11},{3,10},{4,13},{5,12},{6,15},{7,14},{8,17},{9,16... | collective-permute-start | bytes 786440 | tf_op jit(solution)/shard_map/ppermute | solution.py:359
  36.5 1.0 %collective-permute-done.7.theirs = bf16[5,2,2,2,64,256]{5,4,3,2,1,0:T(8,128)(2,1)S(1)} collective-permute-done((bf16[5,2,2,2,64,256]{5,4,3,2,1,0:T(8,128)(2,1)S(1)}, bf16[5,2,2,2,64,256]{5,4,3,2,1,0:T(8,128)(2,1)S(1)}, u32[]{:S(2)}, u32[]{:S(2)}) %collective-permute-start.7) | collective-permute-done | bytes 1310752 | tf_op jit(solution)/shard_map/ppermute | solution.py:331
  37.5 4.8 %forth.1 = (bf16[2,512,512]{2,1,0:T(8,128)(2,1)S(1)}, f32[2,512,512]{2,1,0:T(8,128)S(1)}) custom-call(s32[4]{0:T(128)S(1)} %pad_add_fusion.meta, bf16[5,2,2,2,64,256]{5,4,3,2,1,0:T(8,128)(2,1)S(1)} %bitcast_dynamic-update-slice_fusion.mine, bf16[5,2,2,2,64,256]{5,4,3,2,1,0:T(8,128)(2,1)S(1)} %collective-permute-done.7.theirs, ...), custom_call_target="tpu_custom_call" | custom-call | flops 3221225472 | bytes 262144 | tf_op jit(solution)/shard_map/forth/pallas_call | solution.py:298
  42.3 1.8 %collective-permute-done.8.refs_1_ = bf16[256,512]{1,0:T(8,128)(2,1)S(1)} collective-permute-done((bf16[256,512]{1,0:T(8,128)(2,1)S(1)}, bf16[256,512]{1,0:T(8,128)(2,1)S(1)}, u32[]{:S(2)}, u32[]{:S(2)}) %collective-permute-start.8) | collective-permute-done | bytes 262176 | tf_op jit(solution)/shard_map/ppermute | solution.py:359
  44.0 6.1 %back.1 = (bf16[5,2,2,2,64,256]{5,4,3,2,1,0:T(8,128)(2,1)S(1)}, bf16[5,2,2,2,64,256]{5,4,3,2,1,0:T(8,128)(2,1)S(1)}) custom-call(s32[4]{0:T(128)S(1)} %pad_add_fusion.meta, bf16[5,2,2,2,64,256]{5,4,3,2,1,0:T(8,128)(2,1)S(1)} %bitcast_dynamic-update-slice_fusion.mine, bf16[5,2,2,2,64,256]{5,4,3,2,1,0:T(8,128)(2,1)S(1)} %collective-permute-done.7.theirs, ...), custom_call_target="tpu_custom_call" | custom-call | flops 3221225472 | bytes 262144 | tf_op jit(solution)/shard_map/back/pallas_call | solution.py:298
  50.2 3.0 %collective-permute-done.9 = bf16[5,2,2,2,64,256]{5,4,3,2,1,0:T(8,128)(2,1)S(1)} collective-permute-done((bf16[5,2,2,2,64,256]{5,4,3,2,1,0:T(8,128)(2,1)S(1)}, bf16[5,2,2,2,64,256]{5,4,3,2,1,0:T(8,128)(2,1)S(1)}, u32[]{:S(2)}, u32[]{:S(2)}) %collective-permute-start.9) | collective-permute-done | bytes 1310752 | tf_op jit(solution)/shard_map/ppermute | solution.py:331
  53.9 0.7 collective-permute-start.12
  54.7 4.6 %collective-permute-start.13 = (bf16[2,2,2,64,256]{4,3,2,1,0:T(8,128)(2,1)S(1)}, bf16[2,2,2,64,256]{4,3,2,1,0:T(8,128)(2,1)S(1)}, u32[]{:S(2)}, u32[]{:S(2)}) collective-permute-start(bf16[2,2,2,64,256]{4,3,2,1,0:T(8,128)(2,1)S(1)} %get-tuple-element.29), channel_id=1, source_target_pairs={{0,0},{2,2},{4,8},{6,10},{8,4},{10,6},{12,16},{14,18},{16,12},{18,... | collective-permute-start | bytes 786440 | tf_op jit(solution)/shard_map/ppermute | solution.py:338
  59.3 2.0 %collective-permute-start.11 = (bf16[2,2,2,64,256]{4,3,2,1,0:T(8,128)(2,1)S(1)}, bf16[2,2,2,64,256]{4,3,2,1,0:T(8,128)(2,1)S(1)}, u32[]{:S(2)}, u32[]{:S(2)}) collective-permute-start(bf16[2,2,2,64,256]{4,3,2,1,0:T(8,128)(2,1)S(1)} %get-tuple-element.30), channel_id=1, source_target_pairs={{0,0},{2,2},{4,4},{6,6},{8,16},{10,18},{12,20},{14,22},{16,8},{18,... | collective-permute-start | bytes 786440 | tf_op jit(solution)/shard_map/ppermute | solution.py:338
  61.3 1.0 %collective-permute-done.10 = bf16[2,2,2,64,256]{4,3,2,1,0:T(8,128)(2,1)S(1)} collective-permute-done((bf16[2,2,2,64,256]{4,3,2,1,0:T(8,128)(2,1)S(1)}, bf16[2,2,2,64,256]{4,3,2,1,0:T(8,128)(2,1)S(1)}, u32[]{:S(2)}, u32[]{:S(2)}) %collective-permute-start.10) | collective-permute-done | bytes 262176 | tf_op jit(solution)/shard_map/ppermute | solution.py:331
  62.3 3.9 %collective-permute-done.12 = bf16[2,2,2,64,256]{4,3,2,1,0:T(8,128)(2,1)S(1)} collective-permute-done((bf16[2,2,2,64,256]{4,3,2,1,0:T(8,128)(2,1)S(1)}, bf16[2,2,2,64,256]{4,3,2,1,0:T(8,128)(2,1)S(1)}, u32[]{:S(2)}, u32[]{:S(2)}) %collective-permute-start.12) | collective-permute-done | bytes 262176 | tf_op jit(solution)/shard_map/ppermute | solution.py:331
  66.2 1.8 %collective-permute-done.13 = bf16[2,2,2,64,256]{4,3,2,1,0:T(8,128)(2,1)S(1)} collective-permute-done((bf16[2,2,2,64,256]{4,3,2,1,0:T(8,128)(2,1)S(1)}, bf16[2,2,2,64,256]{4,3,2,1,0:T(8,128)(2,1)S(1)}, u32[]{:S(2)}, u32[]{:S(2)}) %collective-permute-start.13) | collective-permute-done | bytes 262176 | tf_op jit(solution)/shard_map/ppermute | solution.py:338
  68.0 3.1 %collective-permute-done.11 = bf16[2,2,2,64,256]{4,3,2,1,0:T(8,128)(2,1)S(1)} collective-permute-done((bf16[2,2,2,64,256]{4,3,2,1,0:T(8,128)(2,1)S(1)}, bf16[2,2,2,64,256]{4,3,2,1,0:T(8,128)(2,1)S(1)}, u32[]{:S(2)}, u32[]{:S(2)}) %collective-permute-start.11) | collective-permute-done | bytes 262176 | tf_op jit(solution)/shard_map/ppermute | solution.py:338
  71.3 1.1 %collective-permute-start.14 = (bf16[2,2,64,256]{3,2,1,0:T(8,128)(2,1)S(1)}, bf16[2,2,64,256]{3,2,1,0:T(8,128)(2,1)S(1)}, u32[]{:S(2)}, u32[]{:S(2)}) collective-permute-start(bf16[2,2,64,256]{3,2,1,0:T(8,128)(2,1)S(1)} %fusion.2), channel_id=1, source_target_pairs={{0,1},{1,0},{2,3},{3,2},{4,5},{5,4},{6,7},{7,6},{8,9},{9,8},{10,11... | collective-permute-start | bytes 393224 | tf_op jit(solution)/shard_map/ppermute | solution.py:418
  72.3 4.0 %collective-permute-done.14 = bf16[2,2,64,256]{3,2,1,0:T(8,128)(2,1)S(1)} collective-permute-done((bf16[2,2,64,256]{3,2,1,0:T(8,128)(2,1)S(1)}, bf16[2,2,64,256]{3,2,1,0:T(8,128)(2,1)S(1)}, u32[]{:S(2)}, u32[]{:S(2)}) %collective-permute-start.14) | collective-permute-done | bytes 131104 | tf_op jit(solution)/shard_map/ppermute | solution.py:418
  76.3 0.7 bitcast_add_fusion
  (31 shorter events, 5.1 us)
Async XLA Ops:
  0.0 8.2 %copy-start = (bf16[2,512,256]{2,1,0:T(8,128)(2,1)S(1)}, bf16[2,512,256]{2,1,0:T(8,128)(2,1)}, u32[]{:S(2)}) copy-start(bf16[2,512,256]{2,1,0:T(8,128)(2,1)} %refs_0_.1) | copy-start | bytes 1572868
  1.0 7.8 %collective-permute-start.1 = (bf16[2,2,64,256]{3,2,1,0:T(8,128)(2,1)S(1)}, bf16[2,2,64,256]{3,2,1,0:T(8,128)(2,1)}, u32[]{:S(2)}, u32[]{:S(2)}) collective-permute-start(bf16[2,2,64,256]{3,2,1,0:T(8,128)(2,1)S(1)} %convert_element_type.69), channel_id=1, source_target_pairs={{0,1},{1,0},{2,3},{3,2},{4,5},{5,4},{6,7},{7,6},{8,9},{9,8},{10,11... | collective-permute-start | bytes 393224 | tf_op jit(solution)/shard_map/ppermute | solution.py:353
  6.7 11.0 %collective-permute-start = (bf16[272,512]{1,0:T(8,128)(2,1)}, bf16[272,512]{1,0:T(8,128)(2,1)S(1)}, u32[]{:S(2)}, u32[]{:S(2)}) collective-permute-start(bf16[272,512]{1,0:T(8,128)(2,1)} %pad_maximum_fusion), channel_id=1, source_target_pairs={{0,8},{2,10},{4,12},{6,14},{8,16},{10,18},{12,20},{14,22},{16,24},... | collective-permute-start | bytes 835592 | tf_op jit(solution)/shard_map/ppermute | solution.py:328
  8.2 21.1 %collective-permute-start.6 = (bf16[2,512,256]{2,1,0:T(8,128)(2,1)S(1)}, bf16[2,512,256]{2,1,0:T(8,128)(2,1)S(1)}, u32[]{:S(2)}, u32[]{:S(2)}) collective-permute-start(bf16[2,512,256]{2,1,0:T(8,128)(2,1)S(1)} %copy-done), channel_id=1, source_target_pairs={{0,1},{1,0},{2,3},{3,2},{4,5},{5,4},{6,7},{7,6},{8,9},{9,8},{10,11... | collective-permute-start | bytes 1572872 | tf_op jit(solution)/shard_map/ppermute | solution.py:356
  8.8 20.5 %copy-start.1 = (bf16[2,512,512]{2,1,0:T(8,128)(2,1)S(1)}, bf16[2,512,512]{2,1,0:T(8,128)(2,1)}, u32[]{:S(2)}) copy-start(bf16[2,512,512]{2,1,0:T(8,128)(2,1)} %constant.85.clone.far_rows) | copy-start | bytes 3145732
  8.8 20.5 %copy-start.3 = (bf16[2,512,512]{2,1,0:T(8,128)(2,1)S(1)}, bf16[2,512,512]{2,1,0:T(8,128)(2,1)}, u32[]{:S(2)}) copy-start(bf16[2,512,512]{2,1,0:T(8,128)(2,1)} %constant.86.clone.far_cols) | copy-start | bytes 3145732
  10.7 17.5 %collective-permute-start.5 = (bf16[2,2,2,64,256]{4,3,2,1,0:T(8,128)(2,1)}, bf16[2,2,2,64,256]{4,3,2,1,0:T(8,128)(2,1)}, u32[]{:S(2)}, u32[]{:S(2)}) collective-permute-start(bf16[2,2,2,64,256]{4,3,2,1,0:T(8,128)(2,1)} %pad_maximum_fusion.1), channel_id=1, source_target_pairs={{0,0},{2,2},{4,8},{6,10},{8,4},{10,6},{12,16},{14,18},{16,12},{18,... | collective-permute-start | bytes 786440 | tf_op jit(solution)/shard_map/ppermute | solution.py:338
  14.0 14.2 %collective-permute-start.4 = (bf16[2,2,2,64,256]{4,3,2,1,0:T(8,128)(2,1)}, bf16[2,2,2,64,256]{4,3,2,1,0:T(8,128)(2,1)}, u32[]{:S(2)}, u32[]{:S(2)}) collective-permute-start(bf16[2,2,2,64,256]{4,3,2,1,0:T(8,128)(2,1)} %pad_maximum_fusion.1), channel_id=1, source_target_pairs={{0,4},{2,6},{4,0},{6,2},{8,12},{10,14},{12,8},{14,10},{16,20},{18,... | collective-permute-start | bytes 786440 | tf_op jit(solution)/shard_map/ppermute | solution.py:331
  15.7 11.5 %collective-permute-start.3 = (bf16[2,2,2,64,256]{4,3,2,1,0:T(8,128)(2,1)}, bf16[2,2,2,64,256]{4,3,2,1,0:T(8,128)(2,1)}, u32[]{:S(2)}, u32[]{:S(2)}) collective-permute-start(bf16[2,2,2,64,256]{4,3,2,1,0:T(8,128)(2,1)} %pad_maximum_fusion.1), channel_id=1, source_target_pairs={{0,0},{2,2},{4,4},{6,6},{8,16},{10,18},{12,20},{14,22},{16,8},{18,... | collective-permute-start | bytes 786440 | tf_op jit(solution)/shard_map/ppermute | solution.py:338
  17.7 9.5 %collective-permute-start.2 = (bf16[2,2,2,64,256]{4,3,2,1,0:T(8,128)(2,1)}, bf16[2,2,2,64,256]{4,3,2,1,0:T(8,128)(2,1)}, u32[]{:S(2)}, u32[]{:S(2)}) collective-permute-start(bf16[2,2,2,64,256]{4,3,2,1,0:T(8,128)(2,1)} %pad_maximum_fusion.1), channel_id=1, source_target_pairs={{0,8},{2,10},{4,12},{6,14},{8,0},{10,2},{12,4},{14,6},{16,24},{18,... | collective-permute-start | bytes 786440 | tf_op jit(solution)/shard_map/ppermute | solution.py:331
  31.2 3.2 %copy-start.4 = (bf16[256,512]{1,0:T(8,128)(2,1)S(1)}, bf16[256,512]{1,0:T(8,128)(2,1)}, u32[]{:S(2)}) copy-start(bf16[256,512]{1,0:T(8,128)(2,1)} %get-tuple-element.31) | copy-start | bytes 786436
  31.2 6.2 %copy-start.2 = (bf16[2,512,512]{2,1,0:T(8,128)(2,1)S(1)}, bf16[2,512,512]{2,1,0:T(8,128)(2,1)}, u32[]{:S(2)}) copy-start(bf16[2,512,512]{2,1,0:T(8,128)(2,1)} %constant.87.clone.near) | copy-start | bytes 3145732
  34.4 3.1 %collective-permute-start.7 = (bf16[5,2,2,2,64,256]{5,4,3,2,1,0:T(8,128)(2,1)S(1)}, bf16[5,2,2,2,64,256]{5,4,3,2,1,0:T(8,128)(2,1)S(1)}, u32[]{:S(2)}, u32[]{:S(2)}) collective-permute-start(bf16[5,2,2,2,64,256]{5,4,3,2,1,0:T(8,128)(2,1)S(1)} %bitcast_dynamic-update-slice_fusion.mine), channel_id=1, source_target_pairs={{0,2},{2,0},{4,6},{6,4},{8,10},{10,8},{12,14},{14,12},{16,18},{18,... | collective-permute-start | bytes 3932168 | tf_op jit(solution)/shard_map/ppermute | solution.py:331
  34.4 9.6 %collective-permute-start.8 = (bf16[256,512]{1,0:T(8,128)(2,1)S(1)}, bf16[256,512]{1,0:T(8,128)(2,1)S(1)}, u32[]{:S(2)}, u32[]{:S(2)}) collective-permute-start(bf16[256,512]{1,0:T(8,128)(2,1)S(1)} %copy-done.4), channel_id=1, source_target_pairs={{0,9},{1,8},{2,11},{3,10},{4,13},{5,12},{6,15},{7,14},{8,17},{9,16... | collective-permute-start | bytes 786440 | tf_op jit(solution)/shard_map/ppermute | solution.py:359
  50.2 3.1 %collective-permute-start.9 = (bf16[5,2,2,2,64,256]{5,4,3,2,1,0:T(8,128)(2,1)S(1)}, bf16[5,2,2,2,64,256]{5,4,3,2,1,0:T(8,128)(2,1)S(1)}, u32[]{:S(2)}, u32[]{:S(2)}) collective-permute-start(bf16[5,2,2,2,64,256]{5,4,3,2,1,0:T(8,128)(2,1)S(1)} %get-tuple-element.26), channel_id=1, source_target_pairs={{0,2},{2,0},{4,6},{6,4},{8,10},{10,8},{12,14},{14,12},{16,18},{18,... | collective-permute-start | bytes 3932168 | tf_op jit(solution)/shard_map/ppermute | solution.py:331
  53.9 8.4 %collective-permute-start.10 = (bf16[2,2,2,64,256]{4,3,2,1,0:T(8,128)(2,1)S(1)}, bf16[2,2,2,64,256]{4,3,2,1,0:T(8,128)(2,1)S(1)}, u32[]{:S(2)}, u32[]{:S(2)}) collective-permute-start(bf16[2,2,2,64,256]{4,3,2,1,0:T(8,128)(2,1)S(1)} %get-tuple-element.27), channel_id=1, source_target_pairs={{0,8},{2,10},{4,12},{6,14},{8,0},{10,2},{12,4},{14,6},{16,24},{18,... | collective-permute-start | bytes 786440 | tf_op jit(solution)/shard_map/ppermute | solution.py:331
  53.9 12.2 %collective-permute-start.12 = (bf16[2,2,2,64,256]{4,3,2,1,0:T(8,128)(2,1)S(1)}, bf16[2,2,2,64,256]{4,3,2,1,0:T(8,128)(2,1)S(1)}, u32[]{:S(2)}, u32[]{:S(2)}) collective-permute-start(bf16[2,2,2,64,256]{4,3,2,1,0:T(8,128)(2,1)S(1)} %get-tuple-element.28), channel_id=1, source_target_pairs={{0,4},{2,6},{4,0},{6,2},{8,12},{10,14},{12,8},{14,10},{16,20},{18,... | collective-permute-start | bytes 786440 | tf_op jit(solution)/shard_map/ppermute | solution.py:331
  54.7 13.3 %collective-permute-start.13 = (bf16[2,2,2,64,256]{4,3,2,1,0:T(8,128)(2,1)S(1)}, bf16[2,2,2,64,256]{4,3,2,1,0:T(8,128)(2,1)S(1)}, u32[]{:S(2)}, u32[]{:S(2)}) collective-permute-start(bf16[2,2,2,64,256]{4,3,2,1,0:T(8,128)(2,1)S(1)} %get-tuple-element.29), channel_id=1, source_target_pairs={{0,0},{2,2},{4,8},{6,10},{8,4},{10,6},{12,16},{14,18},{16,12},{18,... | collective-permute-start | bytes 786440 | tf_op jit(solution)/shard_map/ppermute | solution.py:338
  59.3 11.8 %collective-permute-start.11 = (bf16[2,2,2,64,256]{4,3,2,1,0:T(8,128)(2,1)S(1)}, bf16[2,2,2,64,256]{4,3,2,1,0:T(8,128)(2,1)S(1)}, u32[]{:S(2)}, u32[]{:S(2)}) collective-permute-start(bf16[2,2,2,64,256]{4,3,2,1,0:T(8,128)(2,1)S(1)} %get-tuple-element.30), channel_id=1, source_target_pairs={{0,0},{2,2},{4,4},{6,6},{8,16},{10,18},{12,20},{14,22},{16,8},{18,... | collective-permute-start | bytes 786440 | tf_op jit(solution)/shard_map/ppermute | solution.py:338
  71.3 5.0 %collective-permute-start.14 = (bf16[2,2,64,256]{3,2,1,0:T(8,128)(2,1)S(1)}, bf16[2,2,64,256]{3,2,1,0:T(8,128)(2,1)S(1)}, u32[]{:S(2)}, u32[]{:S(2)}) collective-permute-start(bf16[2,2,64,256]{3,2,1,0:T(8,128)(2,1)S(1)} %fusion.2), channel_id=1, source_target_pairs={{0,1},{1,0},{2,3},{3,2},{4,5},{5,4},{6,7},{7,6},{8,9},{9,8},{10,11... | collective-permute-start | bytes 393224 | tf_op jit(solution)/shard_map/ppermute | solution.py:418

commit v3 on v2

--- a/solution.py
+++ b/solution.py
@@ -293,6 +293,45 @@
         send[...] = jnp.zeros(send.shape, bf16)
 
 
+def small_call(kernel, out_shape, scalars, values, name):
+    inside = pl.BlockSpec(memory_space=pltpu.VMEM)
+    return pl.pallas_call(
+        kernel,
+        out_shape=out_shape,
+        in_specs=[pl.BlockSpec(memory_space=pltpu.SMEM)] * len(scalars) + [inside] * len(values),
+        out_specs=jax.tree.map(lambda _: inside, out_shape),
+        compiler_params=pltpu.CompilerParams(vmem_limit_bytes=12 * 1024 * 1024),
+        cost_estimate=pl.CostEstimate(flops=0, bytes_accessed=1 << 20, transcendentals=0),
+        name=name,
+    )(*scalars, *values)
+
+
+def placed(values, place_of, name):
+    def kernel(*refs):
+        for number, value in enumerate(refs[:-1]):
+            refs[-1][place_of(number)] = value[...]
+
+    shape = jax.ShapeDtypeStruct((len(values),) + values[0].shape, values[0].dtype)
+    return small_call(kernel, shape, [], values, name)
+
+
+def amplitude_messages(amplitudes, row_offsets, position_counts):
+    slots, rows, size = amplitudes.shape
+
+    def kernel(offsets, counts, amps, straight, crossed):
+        slot = lax.axis_index("scan")
+        straight[0:rows, :] = amps[slot].astype(bf16)
+        crossed[...] = amps[1 - slot].astype(bf16)
+        at = lax.broadcasted_iota(jnp.int32, (16, size), 1)
+        notes = jnp.where(at == slots, counts[0].astype(f32), 0.0)
+        for number in range(slots):
+            notes = jnp.where(at == number, offsets[number].astype(f32), notes)
+        straight[rows : rows + 16, :] = notes.astype(bf16)
+
+    shapes = [jax.ShapeDtypeStruct((n, size), bf16) for n in (rows + 16, rows)]
+    return small_call(kernel, shapes, [row_offsets, position_counts], [amplitudes], "messages")
+
+
 def kernel_call(kernel, size, tile_rows, name, flops, out_shape, meta, *inputs):
     inside = pl.BlockSpec(memory_space=pltpu.VMEM)
     return pl.pallas_call(
@@ -334,7 +373,7 @@
         pairs = []
         for one in range(count):
             step = unit if (one // unit) % 2 else -unit
-            pairs.append((one, one + step if unit <= one < count - unit else one))
+            pairs.append((one, one + step if unit <= one < count - unit else one ^ 1))
         return lax.ppermute(value, "tile", pairs)
 
     def by_slot(first, second):
@@ -347,15 +386,13 @@
 
     own = object_slab.astype(bf16)
     width = own.shape[-1]
-    notes = jnp.concatenate([row_offsets, position_counts]).astype(bf16)
-    notes = jnp.pad(notes[None], ((0, 15), (0, size - slots - 1)))
     if paired:
         beside = lax.ppermute(own, "scan", swap)
-        whole = jnp.stack([by_slot(own, beside), by_slot(beside, own)])
-
+        beside, probe_wave = lax.optimization_barrier((beside, probe_wave))
+        whole = placed([own, beside], lambda n: jnp.bitwise_xor(lax.axis_index("scan"), n), "halves")
         probe_pieces = [probe_wave, lax.ppermute(probe_wave, "scan", swap)]
-        straight, crossed = (by_slot(amplitudes[a], amplitudes[1 - a]).astype(bf16) for a in (0, 1))
-        straight = brought(jnp.concatenate([straight, notes]))
+        straight, crossed = amplitude_messages(amplitudes, row_offsets, position_counts)
+        straight = brought(straight)
         crossed = lax.ppermute(
             crossed,
             ("tile", "scan"),
@@ -367,9 +404,12 @@
         whole = lax.all_gather(own, "scan")
         every = lax.all_gather(probe_wave, "scan")
         probe_pieces = [every[number] for number in range(parts)]
-        notes = brought(notes)[0]
+        notes = brought(jnp.concatenate([row_offsets, position_counts]))
         every = lax.all_gather(brought(amplitudes.astype(bf16)), "scan")
         measured = [every[:, jnp.minimum(slot, slots - 1)].reshape((size, size))]
+    next_across, next_with = paired_across(whole, 4), paired_with(whole, 4)
+    near_across, near_with = paired_across(whole, 2), paired_with(whole, 2)
+    middle, probe_pieces, notes = lax.optimization_barrier((whole, probe_pieces, notes))
     far_rows, far_cols, near = tables(size)
     core = lax.rem(tile, 2)
     notes = notes[: slots + 1].astype(jnp.int32)
@@ -379,17 +419,13 @@
         [notes[jnp.minimum(slot, slots - 1)], live, slot.astype(jnp.int32), core.astype(jnp.int32)]
     )
     turned, far_near, far_far = rolled(probe_pieces, far_rows, far_cols, meta, size)
-    next_across, next_with = paired_across(whole, 4), paired_with(whole, 4)
-    near_across, near_with = paired_across(whole, 2), paired_with(whole, 2)
-    middle, turned = lax.optimization_barrier((whole, turned))
-    arrived = [
-        by_place(4, next_with, next_across),
-        by_place(2, near_with, near_across),
-        middle,
-        by_place(2, near_across, near_with),
-        by_place(4, next_across, next_with),
-    ]
-    mine = jnp.stack(arrived)
+    def group(number):
+        unit, flip = ((4, 0), (2, 1), (2, 2), (2, 3), (4, 4))[number]
+        odd = lax.rem(lax.axis_index("tile") // unit, 2) == 1
+        return jnp.where(odd, flip, 4 - flip)
+
+    arrived = [next_with, near_with, middle, near_across, next_across]
+    mine = placed(arrived, group, "groups")
     theirs = paired_with(mine, 1)
     shape = jax.ShapeDtypeStruct
     psi2, field = kernel_call(

time: 77.7 us -> 76.9 us (0.990)
  the two profiles are of different devices: /device:TPU:8 before, /device:TPU:0 now
where the time goes in v3:
time: 76.9 us; the launch traced here: 75.8 us
  waiting for transfers between devices  35.4 us (46%)
  starting transfers between devices  20.3 us (26%)
  local copies, waits for them, and re-layouts  7.89 us (10%)
  Pallas kernels  6.07 us (8%)
  other arithmetic  4.53 us (6%)
  between operations  1.54 us (2%)
    ppermute x6, waiting for transfers between devices, paired_with(): lax.ppermute(value, 'tile', [(one, one ^ unit) for one in range(count)])  20.9 us
    ppermute x6, starting transfers between devices, paired_with(): lax.ppermute(value, 'tile', [(one, one ^ unit) for one in range(count)])  12.6 us
    unnamed x24, local copies, waits for them, and re-layouts  7.2 us
    ppermute x1, waiting for transfers between devices, brought(): return lax.ppermute(value, 'tile', ahead_pairs)  4.59 us
    ppermute x1, waiting for transfers between devices, shards(): away = lax.ppermute(by_slot(total[1], total[0]).astype(bf16), 'scan', swap)  3.47 us
    ppermute x1, waiting for transfers between devices, shards(): probe_pieces = [probe_wave, lax.ppermute(probe_wave, 'scan', swap)]  3.45 us
    ppermute x1, waiting for transfers between devices, shards(): lax.ppermute(crossed, ('tile', 'scan'), [(2 * a + x, 2 * b + 1 - x) for a...  3.01 us
    ppermute x1, starting transfers between devices, shards(): beside = lax.ppermute(own, 'scan', swap)  3 us
  transfers between devices with their start and end apart: 15, of which 9 were waited for; matrix products, arithmetic and copies ran while one was open for 2% of the time, Pallas kernels for 5%

profile of v3, /device:TPU:0, one launch (start us, length us, event | category | flops | bytes accessed | tf_op | source)
XLA Modules:
  0.0 75.8 jit_solution(15459213277966582598)
XLA Ops:
  0.0 1.0 %convert_element_type.43.refs_0_ = bf16[2,2,64,256]{3,2,1,0:T(8,128)(2,1)S(1)} convert(f32[2,2,64,256]{3,2,1,0:T(8,128)} %param.8) | non-fusion elementwise | flops 65536 | bytes 393216 | tf_op jit(solution)/shard_map/convert_element_type | solution.py:387
  1.0 3.0 %collective-permute-start = (bf16[2,2,64,256]{3,2,1,0:T(8,128)(2,1)S(1)}, bf16[2,2,64,256]{3,2,1,0:T(8,128)(2,1)S(1)}, u32[]{:S(2)}, u32[]{:S(2)}) collective-permute-start(bf16[2,2,64,256]{3,2,1,0:T(8,128)(2,1)S(1)} %convert_element_type.43.refs_0_), channel_id=1, source_target_pairs={{0,1},{1,0},{2,3},{3,2},{4,5},{5,4},{6,7},{7,6},{8,9},{9,8},{10,11... | collective-permute-start | bytes 393224 | tf_op jit(solution)/shard_map/ppermute | solution.py:390
  4.6 1.2 %copy-done = f32[2,256,512]{2,1,0:T(8,128)S(1)} copy-done((f32[2,256,512]{2,1,0:T(8,128)S(1)}, f32[2,256,512]{2,1,0:T(8,128)}, u32[]{:S(2)}) %copy-start) | copy-done | bytes 1048600
  5.9 0.7 copy-done.1
  6.5 1.3 %messages.1 = (bf16[272,512]{1,0:T(8,128)(2,1)S(1)}, bf16[256,512]{1,0:T(8,128)(2,1)}) custom-call(s32[2]{0:T(128)S(1)} %copy-done.1, s32[1]{0:T(128)S(6)} %copy.9.counts, f32[2,256,512]{2,1,0:T(8,128)S(1)} %copy-done), custom_call_target="tpu_custom_call" | custom-call | bytes 1048576 | tf_op jit(solution)/shard_map/messages/pallas_call | solution.py:298
  7.8 1.6 %collective-permute-start.2 = (bf16[272,512]{1,0:T(8,128)(2,1)S(1)}, bf16[272,512]{1,0:T(8,128)(2,1)S(1)}, u32[]{:S(2)}, u32[]{:S(2)}) collective-permute-start(bf16[272,512]{1,0:T(8,128)(2,1)S(1)} %get-tuple-element.24), channel_id=1, source_target_pairs={{0,8},{2,10},{4,12},{6,14},{8,16},{10,18},{12,20},{14,22},{16,24},... | collective-permute-start | bytes 835592 | tf_op jit(solution)/shard_map/ppermute | solution.py:367
  9.4 0.5 collective-permute-start.1
  10.0 0.5 collective-permute-start.5
  10.5 4.1 %collective-permute-start.4 = (bf16[2,2,2,64,256]{4,3,2,1,0:T(8,128)(2,1)S(1)}, bf16[2,2,2,64,256]{4,3,2,1,0:T(8,128)(2,1)S(1)}, u32[]{:S(2)}, u32[]{:S(2)}) collective-permute-start(bf16[2,2,2,64,256]{4,3,2,1,0:T(8,128)(2,1)S(1)} %halves.1.refs_2_), channel_id=1, source_target_pairs={{0,4},{2,6},{4,0},{6,2},{8,12},{10,14},{12,8},{14,10},{16,20},{18,... | collective-permute-start | bytes 786440 | tf_op jit(solution)/shard_map/ppermute | solution.py:370
  14.6 4.6 %collective-permute-done.2.refs_0_ = bf16[272,512]{1,0:T(8,128)(2,1)S(1)} collective-permute-done((bf16[272,512]{1,0:T(8,128)(2,1)S(1)}, bf16[272,512]{1,0:T(8,128)(2,1)S(1)}, u32[]{:S(2)}, u32[]{:S(2)}) %collective-permute-start.2) | collective-permute-done | bytes 278560 | tf_op jit(solution)/shard_map/ppermute | solution.py:367
  19.3 3.4 %collective-permute-done.1.refs_1_ = bf16[2,512,256]{2,1,0:T(8,128)(2,1)S(1)} collective-permute-done((bf16[2,512,256]{2,1,0:T(8,128)(2,1)}, bf16[2,512,256]{2,1,0:T(8,128)(2,1)S(1)}, u32[]{:S(2)}, u32[]{:S(2)}) %collective-permute-start.1) | collective-permute-done | bytes 524320 | tf_op jit(solution)/shard_map/ppermute | solution.py:393
  22.7 1.7 %collective-permute-done.4.refs_1_ = bf16[2,2,2,64,256]{4,3,2,1,0:T(8,128)(2,1)S(1)} collective-permute-done((bf16[2,2,2,64,256]{4,3,2,1,0:T(8,128)(2,1)S(1)}, bf16[2,2,2,64,256]{4,3,2,1,0:T(8,128)(2,1)S(1)}, u32[]{:S(2)}, u32[]{:S(2)}) %collective-permute-start.4) | collective-permute-done | bytes 262176 | tf_op jit(solution)/shard_map/ppermute | solution.py:370
  24.4 4.8 %collective-permute-done.3.refs_0_ = bf16[2,2,2,64,256]{4,3,2,1,0:T(8,128)(2,1)S(1)} collective-permute-done((bf16[2,2,2,64,256]{4,3,2,1,0:T(8,128)(2,1)S(1)}, bf16[2,2,2,64,256]{4,3,2,1,0:T(8,128)(2,1)S(1)}, u32[]{:S(2)}, u32[]{:S(2)}) %collective-permute-start.3) | collective-permute-done | bytes 262176 | tf_op jit(solution)/shard_map/ppermute | solution.py:370
  29.5 0.7 fusion.1
  30.8 0.8 %pad_add_fusion.meta = s32[4]{0:T(128)S(1)} fusion(s32[1]{0:T(128)} %bitcast.3, s32[1]{0:T(128)} %bitcast.2, s32[1]{0:T(128)} %bitcast.1, s32[1]{0:T(128)} %get-tuple-element.43), kind=kLoop, calls=%fused_computation.11 | loop fusion | flops 12 | bytes 32 | tf_op jit(solution)/shard_map/stack | solution.py:418
  31.6 1.0 %copy-done.6 = bf16[2,512,256]{2,1,0:T(8,128)(2,1)S(1)} copy-done((bf16[2,512,256]{2,1,0:T(8,128)(2,1)S(1)}, bf16[2,512,256]{2,1,0:T(8,128)(2,1)}, u32[]{:S(2)}) %copy-start.6) | copy-done | bytes 524312
  32.7 1.2 %copy-done.7 = bf16[2,512,512]{2,1,0:T(8,128)(2,1)S(1)} copy-done((bf16[2,512,512]{2,1,0:T(8,128)(2,1)S(1)}, bf16[2,512,512]{2,1,0:T(8,128)(2,1)}, u32[]{:S(2)}) %copy-start.7) | copy-done | bytes 1048600
  33.9 1.2 %copy-done.10 = bf16[2,512,512]{2,1,0:T(8,128)(2,1)S(1)} copy-done((bf16[2,512,512]{2,1,0:T(8,128)(2,1)S(1)}, bf16[2,512,512]{2,1,0:T(8,128)(2,1)}, u32[]{:S(2)}) %copy-start.10) | copy-done | bytes 1048600
  35.1 1.9 %rolled.1 = (bf16[2,512,512]{2,1,0:T(8,128)(2,1)S(1)}, bf16[2,512,256]{2,1,0:T(8,128)(2,1)S(1)}, bf16[2,256,512]{2,1,0:T(8,128)(2,1)S(1)}) custom-call(s32[4]{0:T(128)S(1)} %pad_add_fusion.meta, bf16[2,512,512]{2,1,0:T(8,128)(2,1)S(1)} %copy-done.7, bf16[2,512,512]{2,1,0:T(8,128)(2,1)S(1)} %copy-done.10, bf16[2,512,256]{2,1,0:T(8,128)(2,1)S(1)} %copy-done.4, ...), custom_call_target="tpu_custom_call" | custom-call | flops 8589934592 | bytes 6291456 | tf_op jit(solution)/shard_map/rolled/pallas_call | solution.py:117
  37.0 0.6 forth.1
  38.1 3.0 %collective-permute-done.8.refs_1_ = bf16[256,512]{1,0:T(8,128)(2,1)} collective-permute-done((bf16[256,512]{1,0:T(8,128)(2,1)}, bf16[256,512]{1,0:T(8,128)(2,1)}, u32[]{:S(2)}, u32[]{:S(2)}) %collective-permute-start.8) | collective-permute-done | bytes 262176 | tf_op jit(solution)/shard_map/ppermute | solution.py:396
  41.1 1.3 %copy-done.3 = bf16[5,2,2,2,64,256]{5,4,3,2,1,0:T(8,128)(2,1)S(1)} copy-done((bf16[5,2,2,2,64,256]{5,4,3,2,1,0:T(8,128)(2,1)S(1)}, bf16[5,2,2,2,64,256]{5,4,3,2,1,0:T(8,128)(2,1)}, u32[]{:S(2)}) %copy-start.3) | copy-done | bytes 1310744
  42.4 2.2 %back.1 = (bf16[5,2,2,2,64,256]{5,4,3,2,1,0:T(8,128)(2,1)S(1)}, bf16[5,2,2,2,64,256]{5,4,3,2,1,0:T(8,128)(2,1)}) custom-call(s32[4]{0:T(128)S(1)} %pad_add_fusion.meta, bf16[5,2,2,2,64,256]{5,4,3,2,1,0:T(8,128)(2,1)S(1)} %groups.1.mine, bf16[5,2,2,2,64,256]{5,4,3,2,1,0:T(8,128)(2,1)S(1)} %copy-done.3, bf16[2,512,512]{2,1,0:T(8,128)(2,1)S(1)} %copy-done.8, ...), custom_call_target="tpu_custom_call" | custom-call | flops 3221225472 | bytes 262144 | tf_op jit(solution)/shard_map/back/pallas_call | solution.py:337
  44.6 3.4 %collective-permute-done.9 = bf16[5,2,2,2,64,256]{5,4,3,2,1,0:T(8,128)(2,1)} collective-permute-done((bf16[5,2,2,2,64,256]{5,4,3,2,1,0:T(8,128)(2,1)}, bf16[5,2,2,2,64,256]{5,4,3,2,1,0:T(8,128)(2,1)}, u32[]{:S(2)}, u32[]{:S(2)}) %collective-permute-start.9) | collective-permute-done | bytes 1310752 | tf_op jit(solution)/shard_map/ppermute | solution.py:370
  48.0 1.8 %add_convert_fusion = bf16[5,2,2,2,64,256]{5,4,3,2,1,0:T(8,128)(2,1)S(1)} fusion(bf16[5,2,2,2,64,256]{5,4,3,2,1,0:T(8,128)(2,1)} %collective-permute-done.9, bf16[5,2,2,2,64,256]{5,4,3,2,1,0:T(8,128)(2,1)S(1)} %get-tuple-element.37), kind=kLoop, calls=%fused_computation | loop fusion | flops 2621440 | bytes 3932160 | tf_op jit(solution)/shard_map/convert_element_type | solution.py:442
  49.9 8.3 %collective-permute-start.10 = (bf16[2,2,2,64,256]{4,3,2,1,0:T(8,128)(2,1)S(1)}, bf16[2,2,2,64,256]{4,3,2,1,0:T(8,128)(2,1)S(1)}, u32[]{:S(2)}, u32[]{:S(2)}) collective-permute-start(bf16[2,2,2,64,256]{4,3,2,1,0:T(8,128)(2,1)S(1)} %get-tuple-element.39), channel_id=1, source_target_pairs={{0,8},{2,10},{4,12},{6,14},{8,0},{10,2},{12,4},{14,6},{16,24},{18,... | collective-permute-start | bytes 786440 | tf_op jit(solution)/shard_map/ppermute | solution.py:370
  58.2 0.5 collective-permute-start.11
  58.7 6.6 %collective-permute-done.10 = bf16[2,2,2,64,256]{4,3,2,1,0:T(8,128)(2,1)S(1)} collective-permute-done((bf16[2,2,2,64,256]{4,3,2,1,0:T(8,128)(2,1)S(1)}, bf16[2,2,2,64,256]{4,3,2,1,0:T(8,128)(2,1)S(1)}, u32[]{:S(2)}, u32[]{:S(2)}) %collective-permute-start.10) | collective-permute-done | bytes 262176 | tf_op jit(solution)/shard_map/ppermute | solution.py:370
  65.3 4.4 %collective-permute-done.12 = bf16[2,2,2,64,256]{4,3,2,1,0:T(8,128)(2,1)S(1)} collective-permute-done((bf16[2,2,2,64,256]{4,3,2,1,0:T(8,128)(2,1)S(1)}, bf16[2,2,2,64,256]{4,3,2,1,0:T(8,128)(2,1)S(1)}, u32[]{:S(2)}, u32[]{:S(2)}) %collective-permute-start.12) | collective-permute-done | bytes 262176 | tf_op jit(solution)/shard_map/ppermute | solution.py:370
  70.0 1.6 %collective-permute-start.14 = (bf16[2,2,64,256]{3,2,1,0:T(8,128)(2,1)S(1)}, bf16[2,2,64,256]{3,2,1,0:T(8,128)(2,1)S(1)}, u32[]{:S(2)}, u32[]{:S(2)}) collective-permute-start(bf16[2,2,64,256]{3,2,1,0:T(8,128)(2,1)S(1)} %fusion), channel_id=1, source_target_pairs={{0,1},{1,0},{2,3},{3,2},{4,5},{5,4},{6,7},{7,6},{8,9},{9,8},{10,11... | collective-permute-start | bytes 393224 | tf_op jit(solution)/shard_map/ppermute | solution.py:454
  71.5 3.5 %collective-permute-done.14 = bf16[2,2,64,256]{3,2,1,0:T(8,128)(2,1)S(1)} collective-permute-done((bf16[2,2,64,256]{3,2,1,0:T(8,128)(2,1)S(1)}, bf16[2,2,64,256]{3,2,1,0:T(8,128)(2,1)S(1)}, u32[]{:S(2)}, u32[]{:S(2)}) %collective-permute-start.14) | collective-permute-done | bytes 131104 | tf_op jit(solution)/shard_map/ppermute | solution.py:454
  75.0 0.8 bitcast_add_fusion
  (38 shorter events, 1.2 us)
Async XLA Ops:
  1.0 8.4 %collective-permute-start = (bf16[2,2,64,256]{3,2,1,0:T(8,128)(2,1)S(1)}, bf16[2,2,64,256]{3,2,1,0:T(8,128)(2,1)S(1)}, u32[]{:S(2)}, u32[]{:S(2)}) collective-permute-start(bf16[2,2,64,256]{3,2,1,0:T(8,128)(2,1)S(1)} %convert_element_type.43.refs_0_), channel_id=1, source_target_pairs={{0,1},{1,0},{2,3},{3,2},{4,5},{5,4},{6,7},{7,6},{8,9},{9,8},{10,11... | collective-permute-start | bytes 393224 | tf_op jit(solution)/shard_map/ppermute | solution.py:390
  4.6 1.2 %copy-start = (f32[2,256,512]{2,1,0:T(8,128)S(1)}, f32[2,256,512]{2,1,0:T(8,128)}, u32[]{:S(2)}) copy-start(f32[2,256,512]{2,1,0:T(8,128)} %amps.1) | copy-start | bytes 3145732
  5.9 0.7 copy-start.1
  7.8 11.4 %collective-permute-start.2 = (bf16[272,512]{1,0:T(8,128)(2,1)S(1)}, bf16[272,512]{1,0:T(8,128)(2,1)S(1)}, u32[]{:S(2)}, u32[]{:S(2)}) collective-permute-start(bf16[272,512]{1,0:T(8,128)(2,1)S(1)} %get-tuple-element.24), channel_id=1, source_target_pairs={{0,8},{2,10},{4,12},{6,14},{8,16},{10,18},{12,20},{14,22},{16,24},... | collective-permute-start | bytes 835592 | tf_op jit(solution)/shard_map/ppermute | solution.py:367
  9.4 13.3 %collective-permute-start.1 = (bf16[2,512,256]{2,1,0:T(8,128)(2,1)}, bf16[2,512,256]{2,1,0:T(8,128)(2,1)S(1)}, u32[]{:S(2)}, u32[]{:S(2)}) collective-permute-start(bf16[2,512,256]{2,1,0:T(8,128)(2,1)} %refs_0_), channel_id=1, source_target_pairs={{0,1},{1,0},{2,3},{3,2},{4,5},{5,4},{6,7},{7,6},{8,9},{9,8},{10,11... | collective-permute-start | bytes 1572872 | tf_op jit(solution)/shard_map/ppermute | solution.py:393
  10.0 12.8 %collective-permute-start.6 = (bf16[2,2,2,64,256]{4,3,2,1,0:T(8,128)(2,1)S(1)}, bf16[2,2,2,64,256]{4,3,2,1,0:T(8,128)(2,1)S(1)}, u32[]{:S(2)}, u32[]{:S(2)}) collective-permute-start(bf16[2,2,2,64,256]{4,3,2,1,0:T(8,128)(2,1)S(1)} %halves.1.refs_2_), channel_id=1, source_target_pairs={{0,2},{2,0},{4,6},{6,4},{8,16},{10,18},{12,20},{14,22},{16,8},{18,... | collective-permute-start | bytes 786440 | tf_op jit(solution)/shard_map/ppermute | solution.py:377
  10.0 12.7 %collective-permute-start.5 = (bf16[2,2,2,64,256]{4,3,2,1,0:T(8,128)(2,1)S(1)}, bf16[2,2,2,64,256]{4,3,2,1,0:T(8,128)(2,1)S(1)}, u32[]{:S(2)}, u32[]{:S(2)}) collective-permute-start(bf16[2,2,2,64,256]{4,3,2,1,0:T(8,128)(2,1)S(1)} %halves.1.refs_2_), channel_id=1, source_target_pairs={{0,2},{2,0},{4,8},{6,10},{8,4},{10,6},{12,16},{14,18},{16,12},{18,... | collective-permute-start | bytes 786440 | tf_op jit(solution)/shard_map/ppermute | solution.py:377
  10.5 13.9 %collective-permute-start.4 = (bf16[2,2,2,64,256]{4,3,2,1,0:T(8,128)(2,1)S(1)}, bf16[2,2,2,64,256]{4,3,2,1,0:T(8,128)(2,1)S(1)}, u32[]{:S(2)}, u32[]{:S(2)}) collective-permute-start(bf16[2,2,2,64,256]{4,3,2,1,0:T(8,128)(2,1)S(1)} %halves.1.refs_2_), channel_id=1, source_target_pairs={{0,4},{2,6},{4,0},{6,2},{8,12},{10,14},{12,8},{14,10},{16,20},{18,... | collective-permute-start | bytes 786440 | tf_op jit(solution)/shard_map/ppermute | solution.py:370
  19.2 9.9 %collective-permute-start.3 = (bf16[2,2,2,64,256]{4,3,2,1,0:T(8,128)(2,1)S(1)}, bf16[2,2,2,64,256]{4,3,2,1,0:T(8,128)(2,1)S(1)}, u32[]{:S(2)}, u32[]{:S(2)}) collective-permute-start(bf16[2,2,2,64,256]{4,3,2,1,0:T(8,128)(2,1)S(1)} %halves.1.refs_2_), channel_id=1, source_target_pairs={{0,8},{2,10},{4,12},{6,14},{8,0},{10,2},{12,4},{14,6},{16,24},{18,... | collective-permute-start | bytes 786440 | tf_op jit(solution)/shard_map/ppermute | solution.py:370
  19.3 12.4 %copy-start.4 = (bf16[2,512,256]{2,1,0:T(8,128)(2,1)S(1)}, bf16[2,512,256]{2,1,0:T(8,128)(2,1)}, u32[]{:S(2)}) copy-start(bf16[2,512,256]{2,1,0:T(8,128)(2,1)} %refs_0_) | copy-start | bytes 1572868
  22.7 6.6 %copy-start.5 = (bf16[2,512,256]{2,1,0:T(8,128)(2,1)}, bf16[2,512,256]{2,1,0:T(8,128)(2,1)S(1)}, u32[]{:S(2)}) copy-start(bf16[2,512,256]{2,1,0:T(8,128)(2,1)S(1)} %collective-permute-done.1.refs_1_) | copy-start | bytes 1572868
  29.3 7.7 %collective-permute-start.7 = (bf16[5,2,2,2,64,256]{5,4,3,2,1,0:T(8,128)(2,1)S(1)}, bf16[5,2,2,2,64,256]{5,4,3,2,1,0:T(8,128)(2,1)S(1)}, u32[]{:S(2)}, u32[]{:S(2)}) collective-permute-start(bf16[5,2,2,2,64,256]{5,4,3,2,1,0:T(8,128)(2,1)S(1)} %groups.1.mine), channel_id=1, source_target_pairs={{0,2},{2,0},{4,6},{6,4},{8,10},{10,8},{12,14},{14,12},{16,18},{18,... | collective-permute-start | bytes 3932168 | tf_op jit(solution)/shard_map/ppermute | solution.py:370
  29.4 11.7 %collective-permute-start.8 = (bf16[256,512]{1,0:T(8,128)(2,1)}, bf16[256,512]{1,0:T(8,128)(2,1)}, u32[]{:S(2)}, u32[]{:S(2)}) collective-permute-start(bf16[256,512]{1,0:T(8,128)(2,1)} %get-tuple-element.33), channel_id=1, source_target_pairs={{0,9},{1,8},{2,11},{3,10},{4,13},{5,12},{6,15},{7,14},{8,17},{9,16... | collective-permute-start | bytes 786440 | tf_op jit(solution)/shard_map/ppermute | solution.py:396
  31.6 1.0 %copy-start.6 = (bf16[2,512,256]{2,1,0:T(8,128)(2,1)S(1)}, bf16[2,512,256]{2,1,0:T(8,128)(2,1)}, u32[]{:S(2)}) copy-start(bf16[2,512,256]{2,1,0:T(8,128)(2,1)} %copy-done.5) | copy-start | bytes 1572868
  32.6 1.2 %copy-start.7 = (bf16[2,512,512]{2,1,0:T(8,128)(2,1)S(1)}, bf16[2,512,512]{2,1,0:T(8,128)(2,1)}, u32[]{:S(2)}) copy-start(bf16[2,512,512]{2,1,0:T(8,128)(2,1)} %constant.66.clone.far_rows) | copy-start | bytes 3145732
  33.9 1.2 %copy-start.10 = (bf16[2,512,512]{2,1,0:T(8,128)(2,1)S(1)}, bf16[2,512,512]{2,1,0:T(8,128)(2,1)}, u32[]{:S(2)}) copy-start(bf16[2,512,512]{2,1,0:T(8,128)(2,1)} %constant.67.clone.far_cols) | copy-start | bytes 3145732
  35.1 1.9 %copy-start.9 = (bf16[2,512,512]{2,1,0:T(8,128)(2,1)S(1)}, bf16[2,512,512]{2,1,0:T(8,128)(2,1)}, u32[]{:S(2)}) copy-start(bf16[2,512,512]{2,1,0:T(8,128)(2,1)} %constant.68.clone.near) | copy-start | bytes 3145732
  35.1 1.9 %copy-start.11 = (bf16[2,512,512]{2,1,0:T(8,128)(2,1)S(1)}, bf16[2,512,512]{2,1,0:T(8,128)(2,1)}, u32[]{:S(2)}) copy-start(bf16[2,512,512]{2,1,0:T(8,128)(2,1)} %constant.67.clone.far_cols) | copy-start | bytes 3145732
  37.0 1.1 %copy-start.2 = (bf16[5,2,2,2,64,256]{5,4,3,2,1,0:T(8,128)(2,1)}, bf16[5,2,2,2,64,256]{5,4,3,2,1,0:T(8,128)(2,1)S(1)}, u32[]{:S(2)}) copy-start(bf16[5,2,2,2,64,256]{5,4,3,2,1,0:T(8,128)(2,1)S(1)} %collective-permute-done.7.theirs) | copy-start | bytes 3932164
  37.0 4.1 %copy-start.8 = (bf16[2,512,512]{2,1,0:T(8,128)(2,1)S(1)}, bf16[2,512,512]{2,1,0:T(8,128)(2,1)}, u32[]{:S(2)}) copy-start(bf16[2,512,512]{2,1,0:T(8,128)(2,1)} %constant.66.clone.far_rows) | copy-start | bytes 3145732
  41.1 1.3 %copy-start.3 = (bf16[5,2,2,2,64,256]{5,4,3,2,1,0:T(8,128)(2,1)S(1)}, bf16[5,2,2,2,64,256]{5,4,3,2,1,0:T(8,128)(2,1)}, u32[]{:S(2)}) copy-start(bf16[5,2,2,2,64,256]{5,4,3,2,1,0:T(8,128)(2,1)} %copy-done.2) | copy-start | bytes 3932164
  44.6 3.4 %collective-permute-start.9 = (bf16[5,2,2,2,64,256]{5,4,3,2,1,0:T(8,128)(2,1)}, bf16[5,2,2,2,64,256]{5,4,3,2,1,0:T(8,128)(2,1)}, u32[]{:S(2)}, u32[]{:S(2)}) collective-permute-start(bf16[5,2,2,2,64,256]{5,4,3,2,1,0:T(8,128)(2,1)} %get-tuple-element.38), channel_id=1, source_target_pairs={{0,2},{2,0},{4,6},{6,4},{8,10},{10,8},{12,14},{14,12},{16,18},{18,... | collective-permute-start | bytes 3932168 | tf_op jit(solution)/shard_map/ppermute | solution.py:370
  49.9 15.4 %collective-permute-start.10 = (bf16[2,2,2,64,256]{4,3,2,1,0:T(8,128)(2,1)S(1)}, bf16[2,2,2,64,256]{4,3,2,1,0:T(8,128)(2,1)S(1)}, u32[]{:S(2)}, u32[]{:S(2)}) collective-permute-start(bf16[2,2,2,64,256]{4,3,2,1,0:T(8,128)(2,1)S(1)} %get-tuple-element.39), channel_id=1, source_target_pairs={{0,8},{2,10},{4,12},{6,14},{8,0},{10,2},{12,4},{14,6},{16,24},{18,... | collective-permute-start | bytes 786440 | tf_op jit(solution)/shard_map/ppermute | solution.py:370
  58.2 11.5 %collective-permute-start.12 = (bf16[2,2,2,64,256]{4,3,2,1,0:T(8,128)(2,1)S(1)}, bf16[2,2,2,64,256]{4,3,2,1,0:T(8,128)(2,1)S(1)}, u32[]{:S(2)}, u32[]{:S(2)}) collective-permute-start(bf16[2,2,2,64,256]{4,3,2,1,0:T(8,128)(2,1)S(1)} %get-tuple-element.40), channel_id=1, source_target_pairs={{0,4},{2,6},{4,0},{6,2},{8,12},{10,14},{12,8},{14,10},{16,20},{18,... | collective-permute-start | bytes 786440 | tf_op jit(solution)/shard_map/ppermute | solution.py:370
  58.2 11.5 %collective-permute-start.13 = (bf16[2,2,2,64,256]{4,3,2,1,0:T(8,128)(2,1)S(1)}, bf16[2,2,2,64,256]{4,3,2,1,0:T(8,128)(2,1)S(1)}, u32[]{:S(2)}, u32[]{:S(2)}) collective-permute-start(bf16[2,2,2,64,256]{4,3,2,1,0:T(8,128)(2,1)S(1)} %get-tuple-element.41), channel_id=1, source_target_pairs={{0,2},{2,0},{4,8},{6,10},{8,4},{10,6},{12,16},{14,18},{16,12},{18,... | collective-permute-start | bytes 786440 | tf_op jit(solution)/shard_map/ppermute | solution.py:377
  58.2 11.5 %collective-permute-start.11 = (bf16[2,2,2,64,256]{4,3,2,1,0:T(8,128)(2,1)S(1)}, bf16[2,2,2,64,256]{4,3,2,1,0:T(8,128)(2,1)S(1)}, u32[]{:S(2)}, u32[]{:S(2)}) collective-permute-start(bf16[2,2,2,64,256]{4,3,2,1,0:T(8,128)(2,1)S(1)} %get-tuple-element.42), channel_id=1, source_target_pairs={{0,2},{2,0},{4,6},{6,4},{8,16},{10,18},{12,20},{14,22},{16,8},{18,... | collective-permute-start | bytes 786440 | tf_op jit(solution)/shard_map/ppermute | solution.py:377
  70.0 5.0 %collective-permute-start.14 = (bf16[2,2,64,256]{3,2,1,0:T(8,128)(2,1)S(1)}, bf16[2,2,64,256]{3,2,1,0:T(8,128)(2,1)S(1)}, u32[]{:S(2)}, u32[]{:S(2)}) collective-permute-start(bf16[2,2,64,256]{3,2,1,0:T(8,128)(2,1)S(1)} %fusion), channel_id=1, source_target_pairs={{0,1},{1,0},{2,3},{3,2},{4,5},{5,4},{6,7},{7,6},{8,9},{9,8},{10,11... | collective-permute-start | bytes 393224 | tf_op jit(solution)/shard_map/ppermute | solution.py:454
